TPU v7x, 512 devices: a whole 4x4x16 slice. The times are simulated.
512 devices in a mesh: expert: 64 (over z, y), dp: 8 (over x, core).
Axes of the slice: x: 4, y: 4, z: 16, core: 2. Of those that a mesh axis runs over, the one named last changes fastest.
Arguments:
- tokens: bfloat16 [2, 2048, 7168], P(None, 'expert'), may hold values from -6 to 6
- routes: int32 [2, 2048, 2], P(None, 'expert'), may hold values from 0 to 3, all different within a row
- mix_weights: float32 [2, 2048, 2], P(None, 'expert'), may hold values from 0.2 to 1
- up_partial: bfloat16 [8, 64, 448, 1024], P('dp', 'expert'), may hold values from -6 to 6
- down_partial: bfloat16 [8, 64, 64, 7168], P('dp', 'expert'), may hold values from -6 to 6
- up_master: float32 [64, 448, 1024], P('expert', None, 'dp'), may hold values from -0.0625 to 0.0625
- down_master: float32 [64, 64, 7168], P('expert', None, 'dp'), may hold values from -0.1875 to 0.1875
- up_first: float32 [64, 448, 1024], P('expert', None, 'dp'), may hold values from -0.0017089844 to 0.0017089844
- down_first: float32 [64, 64, 7168], P('expert', None, 'dp'), may hold values from -0.0017089844 to 0.0017089844
- up_second: float32 [64, 448, 1024], P('expert', None, 'dp'), may hold values from 1e-07 to 1e-06
- down_second: float32 [64, 64, 7168], P('expert', None, 'dp'), may hold values from 1e-07 to 1e-06
- counts: int32 [8, 4], P('dp'), may hold values from 32 to 1023
- owner_key: int32 [1], replicated, may hold values from 0 to 63
Outputs:
- up_update: float32 [64, 448, 1024], P('expert', None, 'dp')
- down_update: float32 [64, 64, 7168], P('expert', None, 'dp')
- decoded: bfloat16 [2, 2048, 7168], P(None, 'expert', 'dp')
Inputs may be any that keep to these rules, and one draw needn't show every extreme that they name: `routes`: each row names 2 different experts.
All inputs are finite; a program needn't handle non-finite values.
Results may differ from a plain program's by a relative error of at most 0.014.
Values may be sent and summed in bfloat16 or wider, within the bound.
A program may use at most 64 MiB of HBM per device.

v0:
```python
import jax
import jax.numpy as jnp
from jax import lax
from jax.sharding import PartitionSpec as P

EXPERTS = 4


beta_one = 0.9
beta_two = 0.95
first_fix = 1.0 - 0.9**10
second_fix = 1.0 - 0.95**10
epsilon = 1e-08
weight_decay = 0.1
learn_rate = 0.001


def partner_2(x, axis, distance):
    return lax.ppermute(x, axis, [(i, i ^ 1 << distance) for i in range(lax.axis_size(axis))])


def adamw_step(gradient, weight, first, second):
    first_new = beta_one * first + (1.0 - beta_one) * gradient
    second_new = beta_two * second + (1.0 - beta_two) * gradient * gradient
    update = (
        first_new / first_fix / (jnp.sqrt(second_new / second_fix) + epsilon)
        + weight_decay * weight
    )
    return (update, weight - learn_rate * update)


def gather_group(piece, replicas):
    position = lax.axis_index("expert")
    holding = piece[None]
    for level in range(replicas.bit_length() - 1):
        partner = partner_2(holding, "expert", level)
        upper = jnp.bitwise_and(jnp.right_shift(position, level), 1)
        holding = jnp.where(
            upper == 1,
            jnp.concatenate([partner, holding], 0),
            jnp.concatenate([holding, partner], 0),
        )
    return holding


def per_device(
    tokens,
    routes,
    mix_weights,
    up_partial,
    down_partial,
    up_master,
    down_master,
    up_first,
    down_first,
    up_second,
    down_second,
    counts,
    owner_key,
):
    peer_count = lax.axis_size("expert")
    replicas = peer_count // EXPERTS
    position = lax.axis_index("expert")
    owner = owner_key[0]
    block = jnp.bitwise_xor(position, owner)
    totals = lax.psum(counts[0], "dp")
    labels = jnp.arange(EXPERTS, dtype=jnp.int32)
    row_count = jnp.sum(jnp.where(labels == block // replicas, totals, 0)).astype(jnp.float32)
    up_sum, down_sum = (
        lax.psum_scatter(up_partial[0, 0], "dp", scatter_dimension=1, tiled=True).astype(
            jnp.float32
        ),
        lax.psum_scatter(down_partial[0, 0], "dp", scatter_dimension=1, tiled=True).astype(
            jnp.float32
        ),
    )
    up_update, up_new = adamw_step(up_sum / row_count, up_master[0], up_first[0], up_second[0])
    down_update, down_new = adamw_step(
        down_sum / row_count, down_master[0], down_first[0], down_second[0]
    )
    piece = jnp.stack(
        [up_new.astype(jnp.bfloat16), down_new.astype(jnp.bfloat16).reshape(up_new.shape)]
    )
    low_bits = replicas.bit_length() - 1
    total_bits = peer_count.bit_length() - 1
    holding = gather_group(piece, replicas)
    for level in range(low_bits, total_bits):
        partner = partner_2(holding, "expert", level)
        holding = jnp.where(
            jnp.bitwise_and(jnp.right_shift(owner, level), 1) == 1, partner, holding
        )
    ordering = jnp.bitwise_xor(jnp.arange(replicas, dtype=jnp.int32), owner % replicas)
    holding = jnp.take(holding, ordering, axis=0)
    model_width = tokens.shape[2]
    up_serve = holding[:, 0].reshape(model_width, up_new.shape[1])
    down_serve = holding[:, 1].reshape(replicas * down_new.shape[0], down_new.shape[1])
    rows_dev = tokens.shape[1]
    slot_count = rows_dev // replicas
    decoded = []
    for step_index in range(tokens.shape[0]):
        chosen = routes[step_index]
        matches = chosen[:, :, None] == labels
        gates = jnp.sum(jnp.where(matches, mix_weights[step_index][:, :, None], 0.0), axis=1)
        routed = jnp.any(matches, axis=1)
        outgoing = jnp.where(
            routed.T[:, :, None], tokens[step_index][None], jnp.zeros((), jnp.bfloat16)
        )
        outgoing = outgoing.reshape(peer_count, slot_count, model_width)
        received = lax.all_to_all(outgoing, "expert", split_axis=0, concat_axis=0, tiled=True)
        flat_rows = received.reshape(-1, model_width)
        hidden = jax.nn.silu(
            jnp.dot(flat_rows, up_serve, preferred_element_type=jnp.float32)
        ).astype(jnp.bfloat16)
        all_units = lax.all_gather(hidden, "dp", axis=1, tiled=True)
        produced = jnp.dot(all_units, down_serve, preferred_element_type=jnp.float32).astype(
            jnp.bfloat16
        )
        produced = produced.reshape(received.shape[0], received.shape[1], produced.shape[1])
        returned = lax.all_to_all(produced, "expert", split_axis=0, concat_axis=0, tiled=True)
        returned = returned.reshape(EXPERTS, rows_dev, returned.shape[2])
        mixed = jnp.einsum("re,erd->rd", gates, returned.astype(jnp.float32))
        decoded.append(mixed.astype(jnp.bfloat16))
    return (up_update[None], down_update[None], jnp.stack(decoded))


def solution(mesh):
    return jax.shard_map(
        per_device,
        mesh=mesh,
        in_specs=(
            P(None, "expert", None),
            P(None, "expert", None),
            P(None, "expert", None),
            P("dp", "expert", None, None),
            P("dp", "expert", None, None),
            P("expert", None, "dp"),
            P("expert", None, "dp"),
            P("expert", None, "dp"),
            P("expert", None, "dp"),
            P("expert", None, "dp"),
            P("expert", None, "dp"),
            P("dp", None),
            P(),
        ),
        out_specs=(P("expert", None, "dp"), P("expert", None, "dp"), P(None, "expert", "dp")),
        check_vma=False,
    )
```

profile of v0, /device:TPU:1, one launch (start us, length us, event | category | flops | bytes accessed | tf_op | source)
XLA Modules:
  0.0 1067.4 jit_solution(11536163070050586693)
XLA Ops:
  7.2 2.7 copy.36
  13.0 3.9 broadcast_in_dim.102
  16.9 2.9 broadcast_select_fusion.4
  19.8 19.4 %all-to-all-start = ((bf16[64,2,7168]{2,1,0:T(2,128)(2,1)}), bf16[64,2,7168]{2,1,0:T(2,128)(2,1)S(1)}, u32[]{:S(2)}, u32[]{:S(2)}) async-start(bf16[64,2,7168]{2,1,0:T(2,128)(2,1)} %broadcast_select_fusion.4), calls=%async_computation | async-start | bytes 3670016 | tf_op jit(solution)/shard_map/all_to_all | solution.py:109
  39.3 8.7 psum.7
  49.9 5.4 reduce-scatter.9.cloned.1.call-done
  57.5 40.0 %reduce-scatter.7.cloned.1.call-done = bf16[128,448]{1,0:T(8,128)(2,1)} async-done(((bf16[1024,448]{1,0:T(8,128)(2,1)}), bf16[128,448]{1,0:T(8,128)(2,1)}) %reduce-scatter.7.cloned.1.call-update) | async-done | bytes 114704
  102.8 6.3 collective-permute-done
  109.2 2.5 collective-permute-start.1
  111.8 12.3 %collective-permute-done.1 = bf16[2,2,448,128]{3,2,1,0:T(8,128)(2,1)} collective-permute-done((bf16[2,2,448,128]{3,2,1,0:T(8,128)(2,1)S(1)}, bf16[2,2,448,128]{3,2,1,0:T(8,128)(2,1)}, u32[]{:S(2)}, u32[]{:S(2)}) %collective-permute-start.1) | collective-permute-done | bytes 458784 | tf_op jit(solution)/shard_map/ppermute | solution.py:19
  127.6 18.7 %collective-permute-done.2 = bf16[4,2,448,128]{3,2,1,0:T(8,128)(2,1)} collective-permute-done((bf16[4,2,448,128]{3,2,1,0:T(8,128)(2,1)S(1)}, bf16[4,2,448,128]{3,2,1,0:T(8,128)(2,1)}, u32[]{:S(2)}, u32[]{:S(2)}) %collective-permute-start.2) | collective-permute-done | bytes 917536 | tf_op jit(solution)/shard_map/ppermute | solution.py:19
  146.3 3.0 maximum_select_fusion.1
  149.3 3.1 collective-permute-start.3
  152.4 81.0 %collective-permute-done.3 = bf16[8,2,448,128]{3,2,1,0:T(8,128)(2,1)} collective-permute-done((bf16[8,2,448,128]{3,2,1,0:T(8,128)(2,1)}, bf16[8,2,448,128]{3,2,1,0:T(8,128)(2,1)}, u32[]{:S(2)}, u32[]{:S(2)}) %collective-permute-start.3) | collective-permute-done | bytes 1835040 | tf_op jit(solution)/shard_map/ppermute | solution.py:19
  233.4 4.8 maximum_select_fusion
  238.2 2.5 collective-permute-start.4
  242.2 4.8 broadcast_in_dim.113
  246.9 4.4 broadcast_select_fusion.1
  251.3 13.0 %all-to-all-start.2 = ((bf16[64,2,7168]{2,1,0:T(2,128)(2,1)}), bf16[64,2,7168]{2,1,0:T(2,128)(2,1)}, u32[]{:S(2)}, u32[]{:S(2)}) async-start(bf16[64,2,7168]{2,1,0:T(2,128)(2,1)} %broadcast_select_fusion.1), calls=%async_computation.2 | async-start | bytes 3670016 | tf_op jit(solution)/shard_map/all_to_all | solution.py:109
  264.3 513.1 %collective-permute-done.4 = bf16[16,2,448,128]{3,2,1,0:T(8,128)(2,1)} collective-permute-done((bf16[16,2,448,128]{3,2,1,0:T(8,128)(2,1)}, bf16[16,2,448,128]{3,2,1,0:T(8,128)(2,1)}, u32[]{:S(2)}, u32[]{:S(2)}) %collective-permute-start.4) | collective-permute-done | bytes 3670048 | tf_op jit(solution)/shard_map/ppermute | solution.py:19
  777.5 4.2 broadcast_select_fusion.2
  781.7 11.2 %collective-permute-start.5 = (bf16[16,2,448,128]{3,2,1,0:T(8,128)(2,1)}, bf16[16,2,448,128]{3,2,1,0:T(8,128)(2,1)}, u32[]{:S(2)}, u32[]{:S(2)}) collective-permute-start(bf16[16,2,448,128]{3,2,1,0:T(8,128)(2,1)} %broadcast_select_fusion.2), channel_id=1, source_target_pairs={{0,256},{8,264},{16,272},{24,280},{32,288},{40,296},{48,304},{56,3... | collective-permute-start | bytes 11010056 | tf_op jit(solution)/shard_map/ppermute | solution.py:19
  794.6 158.3 %collective-permute-done.5 = bf16[16,2,448,128]{3,2,1,0:T(8,128)(2,1)} collective-permute-done((bf16[16,2,448,128]{3,2,1,0:T(8,128)(2,1)}, bf16[16,2,448,128]{3,2,1,0:T(8,128)(2,1)}, u32[]{:S(2)}, u32[]{:S(2)}) %collective-permute-start.5) | collective-permute-done | bytes 3670048 | tf_op jit(solution)/shard_map/ppermute | solution.py:19
  952.9 4.2 broadcast_select_fusion.3
  957.1 4.9 gather_fusion
  966.0 4.4 reshape_squeeze.7
  972.7 23.4 %all_gather.6 = bf16[128,1024]{1,0:T(8,128)(2,1)S(1)} all-gather(bf16[128,128]{1,0:T(8,128)(2,1)S(1)} %multiply_convert_fusion.1), channel_id=1, replica_groups=mesh['expert'=64,'dp'=8] {'dp'}, dimensions={1}, use_global_device_ids=true | all-gather | bytes 294912 | tf_op jit(solution)/shard_map/all_gather | solution.py:114
  997.3 7.9 all-to-all-start.1
  1005.2 4.9 reshape.70
  1012.4 11.9 %all_gather.7 = bf16[128,1024]{1,0:T(8,128)(2,1)S(1)} all-gather(bf16[128,128]{1,0:T(8,128)(2,1)S(1)} %multiply_convert_fusion), channel_id=1, replica_groups=mesh['expert'=64,'dp'=8] {'dp'}, dimensions={1}, use_global_device_ids=true | all-gather | bytes 294912 | tf_op jit(solution)/shard_map/all_gather | solution.py:114
  1025.6 14.8 %all-to-all-start.3 = ((bf16[64,2,896]{2,1,0:T(2,128)(2,1)}), bf16[64,2,896]{2,1,0:T(2,128)(2,1)S(1)}, u32[]{:S(2)}, u32[]{:S(2)}) async-start(bf16[64,2,896]{2,1,0:T(2,128)(2,1)} %reshape.71), calls=%async_computation.3 | async-start | bytes 458752 | tf_op jit(solution)/shard_map/all_to_all | solution.py:119
  1041.1 18.4 %all-to-all-done.3 = bf16[64,2,896]{2,1,0:T(2,128)(2,1)S(1)} async-done(((bf16[64,2,896]{2,1,0:T(2,128)(2,1)}), bf16[64,2,896]{2,1,0:T(2,128)(2,1)S(1)}, u32[]{:S(2)}, u32[]{:S(2)}) %all-to-all-start.3) | async-done | bytes 229408 | tf_op jit(solution)/shard_map/all_to_all | solution.py:119
  (73 shorter events, 30.5 us)
Async XLA Ops:
  7.2 48.2 %reduce-scatter.9.cloned.1.call-start = ((), (), s32[]{:S(2)}) async-start(), calls=%async_computation.7 | async-start | bytes 2064384
  7.2 2.8 copy-start.4
  10.0 1.4 copy-start.9
  10.0 1.6 copy-start.3
  10.0 87.5 %reduce-scatter.7.cloned.1.call-start = ((), (), s32[]{:S(2)}) async-start(), calls=%async_computation.6 | async-start | bytes 1179648
  19.8 19.5 %copy-start.11 = (s32[1,4]{1,0:T(1,128)S(1)}, s32[1,4]{1,0:T(1,128)}, u32[]{:S(2)}) copy-start(s32[1,4]{1,0:T(1,128)} %param.24) | copy-start | bytes 52
  19.8 36.6 %copy-start.5 = (f32[1,64,896]{2,1,0:T(8,128)S(1)}, f32[1,64,896]{2,1,0:T(8,128)}, u32[]{:S(2)}) copy-start(f32[1,64,896]{2,1,0:T(8,128)} %param.19) | copy-start | bytes 688132
  19.8 36.6 %copy-start.6 = (f32[1,64,896]{2,1,0:T(8,128)S(1)}, f32[1,64,896]{2,1,0:T(8,128)}, u32[]{:S(2)}) copy-start(f32[1,64,896]{2,1,0:T(8,128)} %param.23) | copy-start | bytes 688132
  19.8 36.6 %copy-start.7 = (f32[1,64,896]{2,1,0:T(8,128)S(1)}, f32[1,64,896]{2,1,0:T(8,128)}, u32[]{:S(2)}) copy-start(f32[1,64,896]{2,1,0:T(8,128)} %param.21) | copy-start | bytes 688132
  19.8 231.5 %all-to-all-start = ((bf16[64,2,7168]{2,1,0:T(2,128)(2,1)}), bf16[64,2,7168]{2,1,0:T(2,128)(2,1)S(1)}, u32[]{:S(2)}, u32[]{:S(2)}) async-start(bf16[64,2,7168]{2,1,0:T(2,128)(2,1)} %broadcast_select_fusion.4), calls=%async_computation | async-start | bytes 3670016 | tf_op jit(solution)/shard_map/all_to_all | solution.py:109
  39.3 59.3 %copy-start.8 = (f32[1,448,128]{2,1,0:T(8,128)S(1)}, f32[1,448,128]{2,1,0:T(8,128)}, u32[]{:S(2)}) copy-start(f32[1,448,128]{2,1,0:T(8,128)} %param.18) | copy-start | bytes 688132
  100.5 8.6 collective-permute-start
  109.2 2.6 copy-start.2
  109.2 14.8 %collective-permute-start.1 = (bf16[2,2,448,128]{3,2,1,0:T(8,128)(2,1)S(1)}, bf16[2,2,448,128]{3,2,1,0:T(8,128)(2,1)}, u32[]{:S(2)}, u32[]{:S(2)}) collective-permute-start(bf16[2,2,448,128]{3,2,1,0:T(8,128)(2,1)S(1)} %maximum_select_fusion.3), channel_id=1, source_target_pairs={{0,16},{8,24},{16,0},{24,8},{32,48},{40,56},{48,32},{56,40},{64,80... | collective-permute-start | bytes 1376264 | tf_op jit(solution)/shard_map/ppermute | solution.py:19
  125.6 20.7 %collective-permute-start.2 = (bf16[4,2,448,128]{3,2,1,0:T(8,128)(2,1)S(1)}, bf16[4,2,448,128]{3,2,1,0:T(8,128)(2,1)}, u32[]{:S(2)}, u32[]{:S(2)}) collective-permute-start(bf16[4,2,448,128]{3,2,1,0:T(8,128)(2,1)S(1)} %maximum_select_fusion.2), channel_id=1, source_target_pairs={{0,32},{8,40},{16,48},{24,56},{32,0},{40,8},{48,16},{56,24},{64,96... | collective-permute-start | bytes 2752520 | tf_op jit(solution)/shard_map/ppermute | solution.py:19
  149.3 84.0 %collective-permute-start.3 = (bf16[8,2,448,128]{3,2,1,0:T(8,128)(2,1)}, bf16[8,2,448,128]{3,2,1,0:T(8,128)(2,1)}, u32[]{:S(2)}, u32[]{:S(2)}) collective-permute-start(bf16[8,2,448,128]{3,2,1,0:T(8,128)(2,1)} %maximum_select_fusion.1), channel_id=1, source_target_pairs={{0,64},{8,72},{16,80},{24,88},{32,96},{40,104},{48,112},{56,120},{... | collective-permute-start | bytes 5505032 | tf_op jit(solution)/shard_map/ppermute | solution.py:19
  238.2 539.3 %collective-permute-start.4 = (bf16[16,2,448,128]{3,2,1,0:T(8,128)(2,1)}, bf16[16,2,448,128]{3,2,1,0:T(8,128)(2,1)}, u32[]{:S(2)}, u32[]{:S(2)}) collective-permute-start(bf16[16,2,448,128]{3,2,1,0:T(8,128)(2,1)} %maximum_select_fusion), channel_id=1, source_target_pairs={{0,128},{8,136},{16,144},{24,152},{32,160},{40,168},{48,176},{56,1... | collective-permute-start | bytes 11010056 | tf_op jit(solution)/shard_map/ppermute | solution.py:19
  251.3 746.0 %all-to-all-start.2 = ((bf16[64,2,7168]{2,1,0:T(2,128)(2,1)}), bf16[64,2,7168]{2,1,0:T(2,128)(2,1)}, u32[]{:S(2)}, u32[]{:S(2)}) async-start(bf16[64,2,7168]{2,1,0:T(2,128)(2,1)} %broadcast_select_fusion.1), calls=%async_computation.2 | async-start | bytes 3670016 | tf_op jit(solution)/shard_map/all_to_all | solution.py:109
  781.7 171.2 %collective-permute-start.5 = (bf16[16,2,448,128]{3,2,1,0:T(8,128)(2,1)}, bf16[16,2,448,128]{3,2,1,0:T(8,128)(2,1)}, u32[]{:S(2)}, u32[]{:S(2)}) collective-permute-start(bf16[16,2,448,128]{3,2,1,0:T(8,128)(2,1)} %broadcast_select_fusion.2), channel_id=1, source_target_pairs={{0,256},{8,264},{16,272},{24,280},{32,288},{40,296},{48,304},{56,3... | collective-permute-start | bytes 11010056 | tf_op jit(solution)/shard_map/ppermute | solution.py:19
  970.4 25.7 %copy-start = (bf16[1024,896]{1,0:T(8,128)(2,1)S(1)}, bf16[1024,896]{1,0:T(8,128)(2,1)}, u32[]{:S(2)}) copy-start(bf16[1024,896]{1,0:T(8,128)(2,1)} %reshape_squeeze.7) | copy-start | bytes 5505028
  997.3 28.3 %all-to-all-start.1 = ((bf16[64,2,896]{2,1,0:T(2,128)(2,1)}), bf16[64,2,896]{2,1,0:T(2,128)(2,1)S(1)}, u32[]{:S(2)}, u32[]{:S(2)}) async-start(bf16[64,2,896]{2,1,0:T(2,128)(2,1)} %reshape.68), calls=%async_computation.1 | async-start | bytes 458752 | tf_op jit(solution)/shard_map/all_to_all | solution.py:119
  1010.1 14.2 %copy-start.1 = (bf16[1024,896]{1,0:T(8,128)(2,1)S(1)}, bf16[1024,896]{1,0:T(8,128)(2,1)}, u32[]{:S(2)}) copy-start(bf16[1024,896]{1,0:T(8,128)(2,1)} %reshape_squeeze.7) | copy-start | bytes 5505028
  1012.4 28.0 %copy-start.10 = (f32[2,32,2]{1,2,0:T(2,128)S(1)}, f32[2,32,2]{1,2,0:T(2,128)}, u32[]{:S(2)}) copy-start(f32[2,32,2]{1,2,0:T(2,128)} %param.15) | copy-start | bytes 1540
  1025.6 33.9 %all-to-all-start.3 = ((bf16[64,2,896]{2,1,0:T(2,128)(2,1)}), bf16[64,2,896]{2,1,0:T(2,128)(2,1)S(1)}, u32[]{:S(2)}, u32[]{:S(2)}) async-start(bf16[64,2,896]{2,1,0:T(2,128)(2,1)} %reshape.71), calls=%async_computation.3 | async-start | bytes 458752 | tf_op jit(solution)/shard_map/all_to_all | solution.py:119
Sparse Core Ops, SparseCore 0:
  10.9 44.4 reduce-scatter.8
  58.2 39.2 reduce-scatter.6
where the time goes:
time: 1070 us
  waiting for transfers between devices  854 us (80%)
  starting transfers between devices  78.7 us (7%)
  blocking collectives  44 us (4%)
  local copies, waits for them, and re-layouts  37.4 us (3%)
  other arithmetic  31.8 us (3%)
  between operations  15.8 us (1%)
    ppermute x6, waiting for transfers between devices, partner_2(): lax.ppermute(x, axis, [(i, i ^ 1 << distance) for i in range(lax.axis_siz...  790 us
    unnamed x4, waiting for transfers between devices  45.4 us
    all_gather x2, blocking collectives, per_device(): all_units = lax.all_gather(hidden, 'dp', axis=1, tiled=True)  35.3 us
    all_to_all x2, starting transfers between devices, per_device(): lax.all_to_all(outgoing, 'expert', split_axis=0, concat_axis=0, tiled=True)  32.4 us
    ppermute x6, starting transfers between devices, partner_2(): lax.ppermute(x, axis, [(i, i ^ 1 << distance) for i in range(lax.axis_siz...  23.5 us
    all_to_all x2, starting transfers between devices, per_device(): lax.all_to_all(produced, 'expert', split_axis=0, concat_axis=0, tiled=True)  22.7 us
  transfers between devices with their start and end apart: 12, of which 9 were waited for; matrix products, arithmetic and copies ran while one was open for 7% of the time, Pallas kernels for 0%

commit v1 on v0

--- a/solution.py
+++ b/solution.py
@@ -82,13 +82,7 @@
         [up_new.astype(jnp.bfloat16), down_new.astype(jnp.bfloat16).reshape(up_new.shape)]
     )
     low_bits = replicas.bit_length() - 1
-    total_bits = peer_count.bit_length() - 1
     holding = gather_group(piece, replicas)
-    for level in range(low_bits, total_bits):
-        partner = partner_2(holding, "expert", level)
-        holding = jnp.where(
-            jnp.bitwise_and(jnp.right_shift(owner, level), 1) == 1, partner, holding
-        )
     ordering = jnp.bitwise_xor(jnp.arange(replicas, dtype=jnp.int32), owner % replicas)
     holding = jnp.take(holding, ordering, axis=0)
     model_width = tokens.shape[2]
@@ -99,7 +93,7 @@
     decoded = []
     for step_index in range(tokens.shape[0]):
         chosen = routes[step_index]
-        matches = chosen[:, :, None] == labels
+        matches = chosen[:, :, None] == jnp.bitwise_xor(labels, owner // replicas)
         gates = jnp.sum(jnp.where(matches, mix_weights[step_index][:, :, None], 0.0), axis=1)
         routed = jnp.any(matches, axis=1)
         outgoing = jnp.where(

time: 1070 us -> 434 us (0.41)
  waiting for transfers between devices: 854 us -> 242 us
  other arithmetic: 31.8 us -> 18.5 us
    ppermute x6 -> x4, waiting for transfers between devices: 790 us -> 154 us  [partner_2(): lax.ppermute(x, axis, [(i, i ^ 1 << distance) for i in range(lax.axis_siz...]
    all_to_all x2, waiting for transfers between devices: 0.01 us -> 69.2 us  [per_device(): lax.all_to_all(outgoing, 'expert', split_axis=0, concat_axis=0, tiled=True)]
    unnamed x4, waiting for transfers between devices: 45.4 us -> 0.07 us
    all_gather x2, blocking collectives: 35.3 us -> 24.5 us  [per_device(): all_units = lax.all_gather(hidden, 'dp', axis=1, tiled=True)]
    ppermute x6 -> x4, starting transfers between devices: 23.5 us -> 14.1 us  [partner_2(): lax.ppermute(x, axis, [(i, i ^ 1 << distance) for i in range(lax.axis_siz...]
  transfers between devices with their start and end apart: 12 -> 10, of which waited for: 9 -> 6; matrix products, arithmetic and copies ran while one was open for 7% -> 13% of each run, Pallas kernels for 0% -> 0%
where the time goes in v1:
time: 434 us; the launch traced here: 432 us
  waiting for transfers between devices  242 us (56%)
  starting transfers between devices  72.6 us (17%)
  local copies, waits for them, and re-layouts  43.8 us (10%)
  blocking collectives  33.6 us (8%)
  other arithmetic  18.5 us (4%)
  between operations  15.7 us (4%)
  matrix products  6 us (1%)
    ppermute x4, waiting for transfers between devices, partner_2(): lax.ppermute(x, axis, [(i, i ^ 1 << distance) for i in range(lax.axis_siz...  154 us
    all_to_all x2, waiting for transfers between devices, per_device(): lax.all_to_all(outgoing, 'expert', split_axis=0, concat_axis=0, tiled=True)  69.2 us
    all_to_all x2, starting transfers between devices, per_device(): lax.all_to_all(outgoing, 'expert', split_axis=0, concat_axis=0, tiled=True)  29.8 us
    all_to_all x2, starting transfers between devices, per_device(): lax.all_to_all(produced, 'expert', split_axis=0, concat_axis=0, tiled=True)  28.7 us
    all_gather x2, blocking collectives, per_device(): all_units = lax.all_gather(hidden, 'dp', axis=1, tiled=True)  24.5 us
    all_to_all x2, waiting for transfers between devices, per_device(): lax.all_to_all(produced, 'expert', split_axis=0, concat_axis=0, tiled=True)  18.3 us
    ppermute x4, starting transfers between devices, partner_2(): lax.ppermute(x, axis, [(i, i ^ 1 << distance) for i in range(lax.axis_siz...  14.1 us
    broadcast_in_dim x7, local copies, waits for them, and re-layouts, per_device(): jnp.where(routed.T[:, :, None], tokens[step_index][None], jnp.zeros((), j...  12.9 us
  transfers between devices with their start and end apart: 10, of which 6 were waited for; matrix products, arithmetic and copies ran while one was open for 13% of the time, Pallas kernels for 0%

profile of v1, /device:TPU:1, one launch (start us, length us, event | category | flops | bytes accessed | tf_op | source)
XLA Modules:
  0.0 432.2 jit_solution(16788179202410853318)
XLA Ops:
  11.4 3.9 broadcast_in_dim.113
  15.3 2.8 broadcast_select_fusion.1
  18.1 19.3 %all-to-all-start.2 = ((bf16[64,2,7168]{2,1,0:T(2,128)(2,1)}), bf16[64,2,7168]{2,1,0:T(2,128)(2,1)S(1)}, u32[]{:S(2)}, u32[]{:S(2)}) async-start(bf16[64,2,7168]{2,1,0:T(2,128)(2,1)} %broadcast_select_fusion.1), calls=%async_computation.2 | async-start | bytes 3670016 | tf_op jit(solution)/shard_map/all_to_all | solution.py:103
  37.5 2.7 copy.36
  43.2 4.8 %broadcast_in_dim.102 = bf16[64,2,7168]{2,1,0:T(2,128)(2,1)} reshape(bf16[4,32,7168]{2,1,0:T(8,128)(2,1)} %broadcast_in_dim.101) | data formatting | bytes 3670016 | tf_op jit(solution)/shard_map/jit(_where)/broadcast_in_dim | solution.py:99
  47.9 4.4 %broadcast_select_fusion.2 = bf16[64,2,7168]{2,1,0:T(2,128)(2,1)} fusion(bf16[64,2,7168]{2,1,0:T(2,128)(2,1)} %broadcast_in_dim.102, pred[64,2]{1,0:T(8,128)(4,1)S(1)} %broadcast_in_dim.98), kind=kLoop, calls=%fused_computation.4 | loop fusion | flops 917504 | bytes 3670144 | tf_op jit(solution)/shard_map/jit(_where)/select_n | solution.py:99
  52.3 69.2 %all-to-all-done.2 = bf16[64,2,7168]{2,1,0:T(2,128)(2,1)S(1)} async-done(((bf16[64,2,7168]{2,1,0:T(2,128)(2,1)}), bf16[64,2,7168]{2,1,0:T(2,128)(2,1)S(1)}, u32[]{:S(2)}, u32[]{:S(2)}) %all-to-all-start.2) | async-done | bytes 1835040 | tf_op jit(solution)/shard_map/all_to_all | solution.py:103
  122.7 10.5 %all-to-all-start = ((bf16[64,2,7168]{2,1,0:T(2,128)(2,1)}), bf16[64,2,7168]{2,1,0:T(2,128)(2,1)}, u32[]{:S(2)}, u32[]{:S(2)}) async-start(bf16[64,2,7168]{2,1,0:T(2,128)(2,1)} %broadcast_select_fusion.2), calls=%async_computation | async-start | bytes 3670016 | tf_op jit(solution)/shard_map/all_to_all | solution.py:103
  133.2 9.1 %psum.7 = s32[4]{0:T(128)S(1)} all-reduce(s32[4]{0:T(128)S(1)} %bitcast.114), channel_id=1, replica_groups=mesh['expert'=64,'dp'=8] {'dp'}, use_global_device_ids=true, to_apply=%region_1.2 | all-reduce | flops 4 | bytes 32 | tf_op jit(solution)/shard_map/psum | solution.py:66
  147.8 2.8 collective-permute-start
  150.6 5.4 %collective-permute-done = bf16[1,2,448,128]{3,2,1,0:T(8,128)(2,1)S(1)} collective-permute-done((bf16[1,2,448,128]{3,2,1,0:T(8,128)(2,1)S(1)}, bf16[1,2,448,128]{3,2,1,0:T(8,128)(2,1)S(1)}, u32[]{:S(2)}, u32[]{:S(2)}) %collective-permute-start) | collective-permute-done | bytes 229408 | tf_op jit(solution)/shard_map/ppermute | solution.py:19
  156.0 4.3 collective-permute-start.1
  160.4 11.5 %collective-permute-done.1 = bf16[2,2,448,128]{3,2,1,0:T(8,128)(2,1)S(1)} collective-permute-done((bf16[2,2,448,128]{3,2,1,0:T(8,128)(2,1)S(1)}, bf16[2,2,448,128]{3,2,1,0:T(8,128)(2,1)S(1)}, u32[]{:S(2)}, u32[]{:S(2)}) %collective-permute-start.1) | collective-permute-done | bytes 458784 | tf_op jit(solution)/shard_map/ppermute | solution.py:19
  172.0 3.5 collective-permute-start.2
  175.5 57.0 %collective-permute-done.2 = bf16[4,2,448,128]{3,2,1,0:T(8,128)(2,1)} collective-permute-done((bf16[4,2,448,128]{3,2,1,0:T(8,128)(2,1)S(1)}, bf16[4,2,448,128]{3,2,1,0:T(8,128)(2,1)}, u32[]{:S(2)}, u32[]{:S(2)}) %collective-permute-start.2) | collective-permute-done | bytes 917536 | tf_op jit(solution)/shard_map/ppermute | solution.py:19
  232.4 1.7 maximum_select_fusion.1
  234.2 3.5 collective-permute-start.3
  237.7 80.4 %collective-permute-done.3 = bf16[8,2,448,128]{3,2,1,0:T(8,128)(2,1)} collective-permute-done((bf16[8,2,448,128]{3,2,1,0:T(8,128)(2,1)S(1)}, bf16[8,2,448,128]{3,2,1,0:T(8,128)(2,1)}, u32[]{:S(2)}, u32[]{:S(2)}) %collective-permute-start.3) | collective-permute-done | bytes 1835040 | tf_op jit(solution)/shard_map/ppermute | solution.py:19
  318.2 3.6 maximum_select_fusion
  321.8 4.9 %gather_fusion = bf16[16,2,448,128]{3,2,1,0:T(8,128)(2,1)} fusion(bf16[16,2,448,128]{3,2,1,0:T(8,128)(2,1)} %maximum_select_fusion, s32[1024]{0:T(1024)S(1)} %pad_clamp_fusion), kind=kCustom, calls=%fused_computation | custom fusion | bytes 7340096 | tf_op jit(solution)/shard_map/jit(_take)/gather | solution.py:87
  326.7 2.4 broadcast_select_fusion
  329.2 1.5 fusion.29
  330.7 4.4 %reshape_squeeze.7 = bf16[1024,896]{1,0:T(8,128)(2,1)} reshape(bf16[16,1,448,128]{3,2,1,0:T(8,128)(2,1)} %get-tuple-element.11) | data formatting | bytes 3670016 | tf_op jit(solution)/shard_map/reshape;squeeze | solution.py:90
  335.1 4.9 %reshape.74 = bf16[128,7168]{1,0:T(8,128)(2,1)} reshape(bf16[64,2,7168]{2,1,0:T(2,128)(2,1)} %copy-done.2) | data formatting | bytes 3670016 | tf_op jit(solution)/shard_map/reshape | solution.py:104
  340.0 2.3 multiply_convert_fusion
  342.3 12.7 %all_gather.7 = bf16[128,1024]{1,0:T(8,128)(2,1)S(1)} all-gather(bf16[128,128]{1,0:T(8,128)(2,1)S(1)} %multiply_convert_fusion), channel_id=1, replica_groups=mesh['expert'=64,'dp'=8] {'dp'}, dimensions={1}, use_global_device_ids=true | all-gather | bytes 294912 | tf_op jit(solution)/shard_map/all_gather | solution.py:108
  356.3 13.9 %all-to-all-start.3 = ((bf16[64,2,896]{2,1,0:T(2,128)(2,1)}), bf16[64,2,896]{2,1,0:T(2,128)(2,1)S(1)}, u32[]{:S(2)}, u32[]{:S(2)}) async-start(bf16[64,2,896]{2,1,0:T(2,128)(2,1)} %reshape.75), calls=%async_computation.3 | async-start | bytes 458752 | tf_op jit(solution)/shard_map/all_to_all | solution.py:113
  370.2 4.9 %reshape.71 = bf16[128,7168]{1,0:T(8,128)(2,1)} reshape(bf16[64,2,7168]{2,1,0:T(2,128)(2,1)} %all-to-all-done) | data formatting | bytes 3670016 | tf_op jit(solution)/shard_map/reshape | solution.py:104
  375.1 2.3 multiply_convert_fusion.1
  377.4 11.8 %all_gather.6 = bf16[128,1024]{1,0:T(8,128)(2,1)S(1)} all-gather(bf16[128,128]{1,0:T(8,128)(2,1)S(1)} %multiply_convert_fusion.1), channel_id=1, replica_groups=mesh['expert'=64,'dp'=8] {'dp'}, dimensions={1}, use_global_device_ids=true | all-gather | bytes 294912 | tf_op jit(solution)/shard_map/all_gather | solution.py:108
  390.4 14.8 %all-to-all-start.1 = ((bf16[64,2,896]{2,1,0:T(2,128)(2,1)}), bf16[64,2,896]{2,1,0:T(2,128)(2,1)S(1)}, u32[]{:S(2)}, u32[]{:S(2)}) async-start(bf16[64,2,896]{2,1,0:T(2,128)(2,1)} %reshape.72), calls=%async_computation.1 | async-start | bytes 458752 | tf_op jit(solution)/shard_map/all_to_all | solution.py:113
  405.9 18.3 %all-to-all-done.1 = bf16[64,2,896]{2,1,0:T(2,128)(2,1)S(1)} async-done(((bf16[64,2,896]{2,1,0:T(2,128)(2,1)}), bf16[64,2,896]{2,1,0:T(2,128)(2,1)S(1)}, u32[]{:S(2)}, u32[]{:S(2)}) %all-to-all-start.1) | async-done | bytes 229408 | tf_op jit(solution)/shard_map/all_to_all | solution.py:113
  (67 shorter events, 16.9 us)
Async XLA Ops:
  18.1 103.4 %all-to-all-start.2 = ((bf16[64,2,7168]{2,1,0:T(2,128)(2,1)}), bf16[64,2,7168]{2,1,0:T(2,128)(2,1)S(1)}, u32[]{:S(2)}, u32[]{:S(2)}) async-start(bf16[64,2,7168]{2,1,0:T(2,128)(2,1)} %broadcast_select_fusion.1), calls=%async_computation.2 | async-start | bytes 3670016 | tf_op jit(solution)/shard_map/all_to_all | solution.py:103
  37.4 106.2 %reduce-scatter.9.cloned.1.call-start = ((), (), s32[]{:S(2)}) async-start(), calls=%async_computation.7 | async-start | bytes 2064384
  37.5 2.8 copy-start.3
  40.2 105.5 %reduce-scatter.7.cloned.1.call-start = ((), (), s32[]{:S(2)}) async-start(), calls=%async_computation.6 | async-start | bytes 1179648
  52.3 80.9 %copy-start.11 = (s32[1,4]{1,0:T(1,128)S(1)}, s32[1,4]{1,0:T(1,128)}, u32[]{:S(2)}) copy-start(s32[1,4]{1,0:T(1,128)} %param.24) | copy-start | bytes 52
  52.3 92.4 %copy-start.4 = (f32[1,64,896]{2,1,0:T(8,128)S(1)}, f32[1,64,896]{2,1,0:T(8,128)}, u32[]{:S(2)}) copy-start(f32[1,64,896]{2,1,0:T(8,128)} %param.19) | copy-start | bytes 688132
  52.3 92.4 %copy-start.5 = (f32[1,64,896]{2,1,0:T(8,128)S(1)}, f32[1,64,896]{2,1,0:T(8,128)}, u32[]{:S(2)}) copy-start(f32[1,64,896]{2,1,0:T(8,128)} %param.23) | copy-start | bytes 688132
  52.3 92.4 %copy-start.6 = (f32[1,64,896]{2,1,0:T(8,128)S(1)}, f32[1,64,896]{2,1,0:T(8,128)}, u32[]{:S(2)}) copy-start(f32[1,64,896]{2,1,0:T(8,128)} %param.21) | copy-start | bytes 688132
  121.5 1.2 copy-start.2
  122.7 233.5 %all-to-all-start = ((bf16[64,2,7168]{2,1,0:T(2,128)(2,1)}), bf16[64,2,7168]{2,1,0:T(2,128)(2,1)}, u32[]{:S(2)}, u32[]{:S(2)}) async-start(bf16[64,2,7168]{2,1,0:T(2,128)(2,1)} %broadcast_select_fusion.2), calls=%async_computation | async-start | bytes 3670016 | tf_op jit(solution)/shard_map/all_to_all | solution.py:103
  133.2 13.6 %copy-start.7 = (f32[1,448,128]{2,1,0:T(8,128)S(1)}, f32[1,448,128]{2,1,0:T(8,128)}, u32[]{:S(2)}) copy-start(f32[1,448,128]{2,1,0:T(8,128)} %param.18) | copy-start | bytes 688132
  133.2 13.6 %copy-start.8 = (f32[1,448,128]{2,1,0:T(8,128)S(1)}, f32[1,448,128]{2,1,0:T(8,128)}, u32[]{:S(2)}) copy-start(f32[1,448,128]{2,1,0:T(8,128)} %param.22) | copy-start | bytes 688132
  133.2 13.6 %copy-start.9 = (f32[1,448,128]{2,1,0:T(8,128)S(1)}, f32[1,448,128]{2,1,0:T(8,128)}, u32[]{:S(2)}) copy-start(f32[1,448,128]{2,1,0:T(8,128)} %param.20) | copy-start | bytes 688132
  147.8 8.2 %collective-permute-start = (bf16[1,2,448,128]{3,2,1,0:T(8,128)(2,1)S(1)}, bf16[1,2,448,128]{3,2,1,0:T(8,128)(2,1)S(1)}, u32[]{:S(2)}, u32[]{:S(2)}) collective-permute-start(bf16[1,2,448,128]{3,2,1,0:T(8,128)(2,1)S(1)} %maximum_bitcast_fusion), channel_id=1, source_target_pairs={{0,8},{8,0},{16,24},{24,16},{32,40},{40,32},{48,56},{56,48},{64,72... | collective-permute-start | bytes 688136 | tf_op jit(solution)/shard_map/ppermute | solution.py:19
  156.0 15.8 %collective-permute-start.1 = (bf16[2,2,448,128]{3,2,1,0:T(8,128)(2,1)S(1)}, bf16[2,2,448,128]{3,2,1,0:T(8,128)(2,1)S(1)}, u32[]{:S(2)}, u32[]{:S(2)}) collective-permute-start(bf16[2,2,448,128]{3,2,1,0:T(8,128)(2,1)S(1)} %maximum_select_fusion.3), channel_id=1, source_target_pairs={{0,16},{8,24},{16,0},{24,8},{32,48},{40,56},{48,32},{56,40},{64,80... | collective-permute-start | bytes 1376264 | tf_op jit(solution)/shard_map/ppermute | solution.py:19
  172.0 60.5 %collective-permute-start.2 = (bf16[4,2,448,128]{3,2,1,0:T(8,128)(2,1)S(1)}, bf16[4,2,448,128]{3,2,1,0:T(8,128)(2,1)}, u32[]{:S(2)}, u32[]{:S(2)}) collective-permute-start(bf16[4,2,448,128]{3,2,1,0:T(8,128)(2,1)S(1)} %maximum_select_fusion.2), channel_id=1, source_target_pairs={{0,32},{8,40},{16,48},{24,56},{32,0},{40,8},{48,16},{56,24},{64,96... | collective-permute-start | bytes 2752520 | tf_op jit(solution)/shard_map/ppermute | solution.py:19
  234.2 84.0 %collective-permute-start.3 = (bf16[8,2,448,128]{3,2,1,0:T(8,128)(2,1)S(1)}, bf16[8,2,448,128]{3,2,1,0:T(8,128)(2,1)}, u32[]{:S(2)}, u32[]{:S(2)}) collective-permute-start(bf16[8,2,448,128]{3,2,1,0:T(8,128)(2,1)S(1)} %maximum_select_fusion.1), channel_id=1, source_target_pairs={{0,64},{8,72},{16,80},{24,88},{32,96},{40,104},{48,112},{56,120},{... | collective-permute-start | bytes 5505032 | tf_op jit(solution)/shard_map/ppermute | solution.py:19
  340.0 15.0 %copy-start = (bf16[1024,896]{1,0:T(8,128)(2,1)S(1)}, bf16[1024,896]{1,0:T(8,128)(2,1)}, u32[]{:S(2)}) copy-start(bf16[1024,896]{1,0:T(8,128)(2,1)} %reshape_squeeze.7) | copy-start | bytes 5505028
  356.3 34.2 %all-to-all-start.3 = ((bf16[64,2,896]{2,1,0:T(2,128)(2,1)}), bf16[64,2,896]{2,1,0:T(2,128)(2,1)S(1)}, u32[]{:S(2)}, u32[]{:S(2)}) async-start(bf16[64,2,896]{2,1,0:T(2,128)(2,1)} %reshape.75), calls=%async_computation.3 | async-start | bytes 458752 | tf_op jit(solution)/shard_map/all_to_all | solution.py:113
  375.1 14.1 %copy-start.1 = (bf16[1024,896]{1,0:T(8,128)(2,1)S(1)}, bf16[1024,896]{1,0:T(8,128)(2,1)}, u32[]{:S(2)}) copy-start(bf16[1024,896]{1,0:T(8,128)(2,1)} %reshape_squeeze.7) | copy-start | bytes 5505028
  377.4 27.9 %copy-start.10 = (f32[2,32,2]{1,2,0:T(2,128)S(1)}, f32[2,32,2]{1,2,0:T(2,128)}, u32[]{:S(2)}) copy-start(f32[2,32,2]{1,2,0:T(2,128)} %param.15) | copy-start | bytes 1540
  390.4 33.9 %all-to-all-start.1 = ((bf16[64,2,896]{2,1,0:T(2,128)(2,1)}), bf16[64,2,896]{2,1,0:T(2,128)(2,1)S(1)}, u32[]{:S(2)}, u32[]{:S(2)}) async-start(bf16[64,2,896]{2,1,0:T(2,128)(2,1)} %reshape.72), calls=%async_computation.1 | async-start | bytes 458752 | tf_op jit(solution)/shard_map/all_to_all | solution.py:113
Sparse Core Ops, SparseCore 0:
  41.1 40.6 reduce-scatter.8
  84.7 39.2 reduce-scatter.6

commit v2 on v1

v2 whole, which is shorter than its diff:
```python
import functools

import jax
import jax.numpy as jnp
from jax import lax
from jax.experimental import pallas as pl
from jax.experimental.pallas import tpu as pltpu
from jax.sharding import PartitionSpec as P

EXPERTS = 4
LINES = 4
CORES = 2

beta_one = 0.9
beta_two = 0.95
first_fix = 1.0 - 0.9**10
second_fix = 1.0 - 0.95**10
epsilon = 1e-08
weight_decay = 0.1
learn_rate = 0.001


def adamw_step(gradient, weight, first, second):
    first_new = beta_one * first + (1.0 - beta_one) * gradient
    second_new = beta_two * second + (1.0 - beta_two) * gradient * gradient
    update = (
        first_new / first_fix / (jnp.sqrt(second_new / second_fix) + epsilon)
        + weight_decay * weight
    )
    return (update, weight - learn_rate * update)


class Copies:
    def __init__(self, send, recv):
        self.send, self.recv, self.used, self.open = send, recv, 0, []

    def make(self, src, dst, device):
        copy = pltpu.make_async_remote_copy(
            src_ref=src,
            dst_ref=dst,
            send_sem=self.send.at[self.used],
            recv_sem=self.recv.at[self.used],
            device_id=device,
            device_id_type=pl.DeviceIdType.MESH,
        )
        self.used += 1
        self.open.append(copy)
        return copy


def kernel(
    sizes,
    key_ref,
    tokens,
    gates,
    counts,
    up_partial,
    down_partial,
    up_master,
    down_master,
    up_first,
    down_first,
    up_second,
    down_second,
    up_update,
    down_update,
    decoded,
    slabs,
    tok_out,
    tok_in,
    gates_in,
    counts_in,
    up_pair,
    down_pair,
    up_out,
    down_out,
    up_in,
    down_in,
    up_all,
    down_all,
    partial_units,
    swap_out,
    swap_in,
    unit_blocks,
    units_out,
    units_in,
    units_all,
    units_flat,
    back_out,
    back_in,
    send_sems,
    recv_sems,
):
    planes, lines, chips, group, rows, slab, width, units, columns = sizes
    dp_size = chips * CORES
    place = lax.axis_index("expert")
    z, y = place // lines, place % lines
    dp = lax.axis_index("dp")
    x, core = dp // CORES, dp % CORES
    key = key_ref[0]
    key_line = key % lines
    key_plane = key // lines % group
    key_group = key // (lines * group)

    def at_plane(step):
        return ((z + step + planes) % planes * lines + y, dp)

    def at_line(step):
        return (z * lines + (y + step) % lines, dp)

    def at_dp(other):
        return (place, other)

    twin = dp + 1 - 2 * core
    lane = lax.broadcasted_iota(jnp.int32, (rows, 2 * units), 1)
    low = lane < units

    def turn(value):
        return pltpu.roll(value, units, value.ndim - 1)

    partners = (
        [at_plane(1), at_plane(-1)]
        + [at_line(k) for k in range(1, lines)]
        + [at_dp((dp + k) % dp_size) for k in range(1, dp_size)]
    )
    barrier = pltpu.get_barrier_semaphore()
    for partner in partners:
        pl.semaphore_signal(
            barrier, inc=1, device_id=partner, device_id_type=pl.DeviceIdType.MESH
        )
    pl.semaphore_wait(barrier, len(partners))

    copies = Copies(send_sems, recv_sems)

    up_swap, down_swap = [], []
    for chip in range(chips):
        column = pl.multiple_of((chip * CORES + 1 - core) * width, width)
        copy = copies.make(up_partial.at[:, pl.ds(column, width)], up_pair.at[chip], at_dp(twin))
        copy.start()
        up_swap.append(copy)
    counts_moves = []
    for k in range(1, dp_size):
        copy = copies.make(counts, counts_in.at[k], at_dp((dp + k) % dp_size))
        copy.start()
        counts_moves.append(copy)
    for chip in range(chips):
        column = pl.multiple_of((chip * CORES + 1 - core) * columns, columns)
        copy = copies.make(
            down_partial.at[:, pl.ds(column, columns)], down_pair.at[chip], at_dp(twin)
        )
        copy.start()
        down_swap.append(copy)

    for s in range(group * lines):
        slabs[s] = tokens[:, s * slab : (s + 1) * slab]
    for line in range(lines):
        for plane in range(group):
            which = jnp.bitwise_xor(plane, key_plane) * lines + jnp.bitwise_xor(line, key_line)
            tok_out[line, plane] = slabs[which]
    token_moves = []
    for k in range(1, lines):
        copy = copies.make(tok_out.at[(y + k) % lines], tok_in.at[y], at_line(k))
        copy.start()
        token_moves.append(copy)
        copy = copies.make(gates, gates_in.at[y], at_line(k))
        copy.start()
        token_moves.append(copy)
    tok_in[y] = tok_out[y]
    gates_in[y] = gates[...]

    up_moves, down_moves = [], []

    def pair_sum(partial, pair, chip, extent):
        column = pl.multiple_of((chip * CORES + core) * extent, extent)
        return partial[:, pl.ds(column, extent)].astype(jnp.float32) + pair[chip].astype(
            jnp.float32
        )

    for copy in up_swap:
        copy.wait_recv()
    for k in range(1, chips):
        chip = (x + k) % chips
        up_out[k] = pair_sum(up_partial, up_pair, chip, width).astype(jnp.bfloat16)
        copy = copies.make(up_out.at[k], up_in.at[k], at_dp(chip * CORES + core))
        copy.start()
        up_moves.append(copy)
    for copy in down_swap:
        copy.wait_recv()
    for k in range(1, chips):
        chip = (x + k) % chips
        down_out[k] = pair_sum(down_partial, down_pair, chip, columns).astype(jnp.bfloat16)
        copy = copies.make(down_out.at[k], down_in.at[k], at_dp(chip * CORES + core))
        copy.start()
        down_moves.append(copy)

    for copy in counts_moves:
        copy.wait_recv()
    totals = counts[...].astype(jnp.float32)
    for k in range(1, dp_size):
        totals = totals + counts_in[k].astype(jnp.float32)
    owner = jnp.bitwise_xor(z // group, key_group)
    label = lax.broadcasted_iota(jnp.int32, totals.shape, 1)
    row_count = jnp.sum(jnp.where(label == owner, totals, 0.0))

    up_total = pair_sum(up_partial, up_pair, x, width)
    for copy in up_moves:
        copy.wait_recv()
    for k in range(1, chips):
        up_total = up_total + up_in[k].astype(jnp.float32)
    update, new = adamw_step(up_total / row_count, up_master[...], up_first[...], up_second[...])
    up_update[...] = update
    up_all[z] = new.astype(jnp.bfloat16)

    farthest = planes // 2

    def ring(blocks, extent):
        half = extent // 2
        steps = {}
        for step in range(1, farthest + 1):
            steps[step] = []
            for way, part in ((1, 0), (-1, 1), (1, 1), (-1, 0)):
                if step == farthest and (way == 1) != (part == 0):
                    continue
                block = (z - way * (step - 1) + planes) % planes
                ref = blocks.at[block, pl.ds(part * half, half)]
                steps[step].append(copies.make(ref, ref, at_plane(way)))
        return steps

    def send(steps, step):
        for copy in steps[step]:
            copy.start()

    def pass_on(steps, step):
        onward = steps.get(step + 1, [])
        for at, copy in enumerate(steps[step]):
            copy.wait_recv()
            if at < len(onward):
                onward[at].start()

    up_ring = ring(up_all, slab)
    down_ring = ring(down_all, units)

    def meet(block):
        held = tok_in[:, block % group].reshape(lines * rows, slab)
        product = jnp.dot(held, up_all[block], preferred_element_type=jnp.float32)
        partial_units[block // group] = partial_units[block // group] + product

    def meet_step(step):
        meet((z - step + planes) % planes)
        if step < farthest:
            meet((z + step) % planes)

    send(up_ring, 1)
    partial_units[...] = jnp.zeros_like(partial_units)

    down_total = pair_sum(down_partial, down_pair, x, columns)
    for copy in down_moves:
        copy.wait_recv()
    for k in range(1, chips):
        down_total = down_total + down_in[k].astype(jnp.float32)
    update, new = adamw_step(
        down_total / row_count, down_master[...], down_first[...], down_second[...]
    )
    down_update[...] = update
    down_all[z] = new.astype(jnp.bfloat16)

    for copy in token_moves:
        copy.wait_recv()
    pass_on(up_ring, 1)
    meet(z)
    meet_step(1)
    for step in range(2, farthest - 1):
        pass_on(up_ring, step)
        meet_step(step)
    send(down_ring, 1)
    pass_on(up_ring, farthest - 1)
    meet_step(farthest - 1)
    pass_on(up_ring, farthest)
    meet_step(farthest)

    half = lines * rows // 2
    swap_out[...] = partial_units[:, pl.ds(pl.multiple_of((1 - core) * half, half), half)].astype(
        jnp.bfloat16
    )
    swap = copies.make(swap_out, swap_in, at_dp(twin))
    swap.start()
    pass_on(down_ring, 1)
    swap.wait_recv()

    def blocks_of(value, first):
        upper, lower = value[:, :rows], value[:, rows:]
        unit_blocks[first] = jnp.where(low, upper, turn(lower))
        unit_blocks[first + 1] = jnp.where(low, turn(upper), lower)

    blocks_of(partial_units[:, pl.ds(pl.multiple_of(core * half, half), half)], 2 * core)
    blocks_of(swap_in[...].astype(jnp.float32), 2 * (1 - core))
    unit_moves = []
    for k in range(1, lines):
        line = (y + k) % lines
        units_out[k] = unit_blocks[jnp.bitwise_xor(line, key_line)].astype(jnp.bfloat16)
        copy = copies.make(units_out.at[k], units_in.at[k], at_line(k))
        copy.start()
        unit_moves.append(copy)
    pass_on(down_ring, 2)
    summed = unit_blocks[jnp.bitwise_xor(y, key_line)]
    for copy in unit_moves:
        copy.wait_recv()
    for k in range(1, lines):
        summed = summed + units_in[k].astype(jnp.float32)
    for g in range(EXPERTS):
        upper = gates_in[2 * core][:, g : g + 1]
        lower = gates_in[2 * core + 1][:, g : g + 1]
        gate = jnp.where(low, upper, lower)
        units_all[dp, g] = (jax.nn.silu(summed[g]) * gate).astype(jnp.bfloat16)
    spread = []
    for k in range(1, dp_size):
        copy = copies.make(units_all.at[dp], units_all.at[dp], at_dp((dp + k) % dp_size))
        copy.start()
        spread.append(copy)
    for step in range(3, farthest - 1):
        pass_on(down_ring, step)
    for copy in spread:
        copy.wait_recv()

    for g in range(EXPERTS):
        for pair in range(group // 2):
            column = (g * group + 2 * pair) * units
            for owner_core in range(CORES):
                even = units_all[
                    jnp.bitwise_xor(2 * pair, key_plane) * CORES + owner_core, g
                ].astype(jnp.float32)
                odd = units_all[
                    jnp.bitwise_xor(2 * pair + 1, key_plane) * CORES + owner_core, g
                ].astype(jnp.float32)
                row = owner_core * half
                units_flat[row : row + rows, column : column + 2 * units] = jnp.where(
                    low, even, turn(odd)
                ).astype(jnp.bfloat16)
                units_flat[row + rows : row + half, column : column + 2 * units] = jnp.where(
                    low, turn(even), odd
                ).astype(jnp.bfloat16)
    for step in range(farthest - 1, farthest + 1):
        pass_on(down_ring, step)

    flat_down = down_all[...].reshape(planes * units, columns)

    def produce(line):
        held = units_flat[pl.ds(pl.multiple_of(line * rows, rows), rows)]
        return jnp.dot(held, flat_down, preferred_element_type=jnp.float32)

    back_moves = []
    for k in range(1, lines):
        back_out[k] = produce((y + k) % lines).astype(jnp.bfloat16)
        copy = copies.make(back_out.at[k], back_in.at[k], at_line(k))
        copy.start()
        back_moves.append(copy)
    result = produce(y)
    for copy in back_moves:
        copy.wait_recv()
    for k in range(1, lines):
        result = result + back_in[k].astype(jnp.float32)
    decoded[...] = result.astype(jnp.bfloat16)

    for copy in copies.open:
        copy.wait_send()


def per_device(
    tokens,
    routes,
    mix_weights,
    up_partial,
    down_partial,
    up_master,
    down_master,
    up_first,
    down_first,
    up_second,
    down_second,
    counts,
    owner_key,
):
    planes = lax.axis_size("expert") // LINES
    dp_size = lax.axis_size("dp")
    chips = dp_size // CORES
    group = planes // EXPERTS
    steps, rows_dev, model = tokens.shape
    rows = steps * rows_dev
    slab, width = up_master.shape[1:]
    units, columns = down_master.shape[1:]
    bf16, f32 = jnp.bfloat16, jnp.float32

    holder = jnp.bitwise_xor(
        jnp.arange(EXPERTS, dtype=jnp.int32), owner_key[0] // (LINES * group)
    )
    matches = routes[..., None] == holder
    gates = jnp.sum(jnp.where(matches, mix_weights[..., None], 0.0), axis=2)
    gates = jnp.pad(gates.reshape(rows, EXPERTS), ((0, 0), (0, 128 - EXPERTS)))
    counts = jnp.pad(counts, ((0, 7), (0, 128 - EXPERTS)))

    copies = (
        2 * chips
        + (dp_size - 1)
        + 2 * (LINES - 1)
        + 2 * (chips - 1)
        + 2 * 2 * (planes - 1)
        + 1
        + (LINES - 1)
        + (dp_size - 1)
        + (LINES - 1)
    )
    scratch = [
        pltpu.VMEM((group * LINES, rows, slab), bf16),
        pltpu.VMEM((LINES, group, rows, slab), bf16),
        pltpu.VMEM((LINES, group, rows, slab), bf16),
        pltpu.VMEM((LINES, rows, 128), f32),
        pltpu.VMEM((dp_size, 8, 128), jnp.int32),
        pltpu.VMEM((chips, slab, width), bf16),
        pltpu.VMEM((chips, units, columns), bf16),
        pltpu.VMEM((chips, slab, width), bf16),
        pltpu.VMEM((chips, units, columns), bf16),
        pltpu.VMEM((chips, slab, width), bf16),
        pltpu.VMEM((chips, units, columns), bf16),
        pltpu.VMEM((planes, slab, width), bf16),
        pltpu.VMEM((planes, units, columns), bf16),
        pltpu.VMEM((EXPERTS, LINES * rows, width), f32),
        pltpu.VMEM((EXPERTS, LINES * rows // 2, width), bf16),
        pltpu.VMEM((EXPERTS, LINES * rows // 2, width), bf16),
        pltpu.VMEM((LINES, EXPERTS, rows, 2 * units), f32),
        pltpu.VMEM((LINES, EXPERTS, rows, 2 * units), bf16),
        pltpu.VMEM((LINES, EXPERTS, rows, 2 * units), bf16),
        pltpu.VMEM((dp_size, EXPERTS, rows, 2 * units), bf16),
        pltpu.VMEM((LINES * rows, planes * units), bf16),
        pltpu.VMEM((LINES, rows, columns), bf16),
        pltpu.VMEM((LINES, rows, columns), bf16),
        pltpu.SemaphoreType.DMA((copies,)),
        pltpu.SemaphoreType.DMA((copies,)),
    ]
    vmem = pl.BlockSpec(memory_space=pltpu.VMEM)
    sizes = (planes, LINES, chips, group, rows, slab, width, units, columns)
    up_update, down_update, decoded = pl.pallas_call(
        functools.partial(kernel, sizes),
        out_shape=(
            jax.ShapeDtypeStruct((slab, width), f32),
            jax.ShapeDtypeStruct((units, columns), f32),
            jax.ShapeDtypeStruct((rows, columns), bf16),
        ),
        in_specs=[pl.BlockSpec(memory_space=pltpu.SMEM)] + [vmem] * 11,
        out_specs=(vmem, vmem, vmem),
        scratch_shapes=scratch,
        compiler_params=pltpu.CompilerParams(
            collective_id=0, has_side_effects=True, vmem_limit_bytes=48 * 1024 * 1024
        ),
        cost_estimate=pl.CostEstimate(
            flops=2 * 2 * LINES * rows * planes * slab * width,
            bytes_accessed=6 * 1024 * 1024,
            transcendentals=0,
        ),
    )(
        owner_key,
        tokens.reshape(rows, model),
        gates,
        counts,
        up_partial[0, 0],
        down_partial[0, 0],
        up_master[0],
        down_master[0],
        up_first[0],
        down_first[0],
        up_second[0],
        down_second[0],
    )
    return (up_update[None], down_update[None], decoded.reshape(steps, rows_dev, columns))


def solution(mesh):
    return jax.shard_map(
        per_device,
        mesh=mesh,
        in_specs=(
            P(None, "expert", None),
            P(None, "expert", None),
            P(None, "expert", None),
            P("dp", "expert", None, None),
            P("dp", "expert", None, None),
            P("expert", None, "dp"),
            P("expert", None, "dp"),
            P("expert", None, "dp"),
            P("expert", None, "dp"),
            P("expert", None, "dp"),
            P("expert", None, "dp"),
            P("dp", None),
            P(),
        ),
        out_specs=(P("expert", None, "dp"), P("expert", None, "dp"), P(None, "expert", "dp")),
        check_vma=False,
    )
```

time: 434 us -> 104 us (0.24)
  the two profiles are of different devices: /device:TPU:1 before, /device:TPU:32 now
where the time goes in v2:
time: 104 us
  Pallas kernels  89.7 us (86%)
  local copies, waits for them, and re-layouts  12.5 us (12%)
  between operations  1.35 us (1%)
    pallas_call x1, Pallas kernels, per_device(): pl.pallas_call(functools.partial(kernel, sizes), out_shape=(jax.ShapeDtyp...  89.7 us
    unnamed x27, local copies, waits for them, and re-layouts  12.4 us

profile of v2, /device:TPU:32, one launch (start us, length us, event | category | flops | bytes accessed | tf_op | source)
XLA Modules:
  0.0 103.7 jit_solution(9953995977309030873)
XLA Ops:
  1.3 0.0 copy-start.10
  1.3 0.0 copy-start.9
  1.3 0.7 copy-done.10
  2.0 0.0 copy-done.9
  2.0 0.0 copy-start.11
  2.0 0.1 select_reduce_fusion
  2.1 0.6 copy-done.11
  2.7 0.1 copy.18
  2.8 0.0 copy-start
  2.8 1.2 %copy-done = bf16[2,32,7168]{2,1,0:T(8,128)(2,1)S(1)} copy-done((bf16[2,32,7168]{2,1,0:T(8,128)(2,1)S(1)}, bf16[2,32,7168]{2,1,0:T(8,128)(2,1)}, u32[]{:S(2)}) %copy-start) | copy-done | bytes 917528
  4.0 0.0 copy-start.1
  4.0 1.2 %copy-done.1 = bf16[1,1,448,1024]{3,2,1,0:T(8,128)(2,1)S(1)} copy-done((bf16[1,1,448,1024]{3,2,1,0:T(8,128)(2,1)S(1)}, bf16[1,1,448,1024]{3,2,1,0:T(8,128)(2,1)}, u32[]{:S(2)}) %copy-start.1) | copy-done | bytes 917528
  5.1 0.0 copy-start.2
  5.1 1.2 %copy-done.2 = bf16[1,1,64,7168]{3,2,1,0:T(8,128)(2,1)S(1)} copy-done((bf16[1,1,64,7168]{3,2,1,0:T(8,128)(2,1)S(1)}, bf16[1,1,64,7168]{3,2,1,0:T(8,128)(2,1)}, u32[]{:S(2)}) %copy-start.2) | copy-done | bytes 917528
  6.3 0.0 copy-start.3
  6.3 0.9 copy-done.3
  7.3 0.0 copy-start.4
  7.3 0.9 copy-done.4
  8.2 0.0 copy-start.5
  8.2 0.9 copy-done.5
  9.1 0.0 copy-start.6
  9.1 0.9 copy-done.6
  10.1 0.0 copy-start.7
  10.1 0.9 copy-done.7
  11.0 0.0 copy-start.8
  11.0 0.9 copy-done.8
  11.9 89.7 %shard_map.148 = (f32[448,128]{1,0:T(8,128)S(1)}, f32[64,896]{1,0:T(8,128)S(1)}, bf16[64,896]{1,0:T(8,128)(2,1)S(1)}) custom-call(s32[1]{0:T(128)} %copy.22.key_ref, bf16[64,7168]{1,0:T(8,128)(2,1)S(1)} %bitcast.18, f32[64,128]{1,0:T(8,128)S(1)} %pad.8.gates, s32[8,128]{1,0:T(8,128)S(1)} %pad.9.counts, bf16[448,1024]{1,0:T(8,128)(2,1)S(1)} %bitcast.19, ...), custom_call_target="tpu_custom_call" | custom-call | flops 939524096 | bytes 6291456 | tf_op jit(solution)/shard_map/pallas_call | solution.py:441
  101.6 0.7 copy.23
  102.3 0.7 copy.24
  103.0 0.6 copy.25
  (3 shorter events, 0.0 us)
Async XLA Ops:
  1.3 0.7 copy-start.10
  1.3 0.7 copy-start.9
  2.0 0.7 copy-start.11
  2.8 1.2 %copy-start = (bf16[2,32,7168]{2,1,0:T(8,128)(2,1)S(1)}, bf16[2,32,7168]{2,1,0:T(8,128)(2,1)}, u32[]{:S(2)}) copy-start(bf16[2,32,7168]{2,1,0:T(8,128)(2,1)} %param.13) | copy-start | bytes 2752516
  4.0 1.2 %copy-start.1 = (bf16[1,1,448,1024]{3,2,1,0:T(8,128)(2,1)S(1)}, bf16[1,1,448,1024]{3,2,1,0:T(8,128)(2,1)}, u32[]{:S(2)}) copy-start(bf16[1,1,448,1024]{3,2,1,0:T(8,128)(2,1)} %param.16) | copy-start | bytes 2752516
  5.1 1.2 %copy-start.2 = (bf16[1,1,64,7168]{3,2,1,0:T(8,128)(2,1)S(1)}, bf16[1,1,64,7168]{3,2,1,0:T(8,128)(2,1)}, u32[]{:S(2)}) copy-start(bf16[1,1,64,7168]{3,2,1,0:T(8,128)(2,1)} %param.17) | copy-start | bytes 2752516
  6.3 0.9 copy-start.3
  7.3 0.9 copy-start.4
  8.2 0.9 copy-start.5
  9.1 0.9 copy-start.6
  10.1 0.9 copy-start.7
  11.0 0.9 copy-start.8

commit v3 on v2

--- a/solution.py
+++ b/solution.py
@@ -30,32 +30,66 @@
     return (update, weight - learn_rate * update)
 
 
+class Copy:
+    def __init__(self, copy):
+        self.copy, self.started, self.landed = copy, False, False
+
+    def start(self):
+        self.copy.start()
+        self.started = True
+
+    def wait_recv(self):
+        self.copy.wait_recv()
+        self.landed = True
+
+
 class Copies:
     def __init__(self, send, recv):
-        self.send, self.recv, self.used, self.open = send, recv, 0, []
+        self.send, self.recv, self.made = send, recv, []
 
     def make(self, src, dst, device):
-        copy = pltpu.make_async_remote_copy(
-            src_ref=src,
-            dst_ref=dst,
-            send_sem=self.send.at[self.used],
-            recv_sem=self.recv.at[self.used],
-            device_id=device,
-            device_id_type=pl.DeviceIdType.MESH,
+        at = len(self.made)
+        copy = Copy(
+            pltpu.make_async_remote_copy(
+                src_ref=src,
+                dst_ref=dst,
+                send_sem=self.send.at[at],
+                recv_sem=self.recv.at[at],
+                device_id=device,
+                device_id_type=pl.DeviceIdType.MESH,
+            )
         )
-        self.used += 1
-        self.open.append(copy)
+        self.made.append(copy)
         return copy
+
+    def drain(self):
+        for copy in self.made:
+            if copy.started:
+                copy.copy.wait_send()
+                if not copy.landed:
+                    copy.copy.wait_recv()
 
 
 def kernel(
     sizes,
     key_ref,
-    tokens,
     gates,
     counts,
+    tokens_far,
     up_partial,
     down_partial,
+    up_master_far,
+    down_master_far,
+    up_first_far,
+    down_first_far,
+    up_second_far,
+    down_second_far,
+    up_update_far,
+    down_update_far,
+    decoded_far,
+    tokens,
+    up_own,
+    down_own,
     up_master,
     down_master,
     up_first,
@@ -90,6 +124,7 @@
     back_in,
     send_sems,
     recv_sems,
+    local_sems,
 ):
     planes, lines, chips, group, rows, slab, width, units, columns = sizes
     dp_size = chips * CORES
@@ -118,6 +153,34 @@
     def turn(value):
         return pltpu.roll(value, units, value.ndim - 1)
 
+    def local(src, dst, at):
+        copy = pltpu.make_async_copy(src, dst, local_sems.at[at])
+        copy.start()
+        return copy
+
+    tokens_load = local(tokens_far, tokens, 0)
+    up_loads, down_loads = [], []
+    for chip in range(chips):
+        column = pl.multiple_of((chip * CORES + core) * width, width)
+        up_loads.append(local(up_partial.at[:, pl.ds(column, width)], up_own.at[chip], 1 + chip))
+    for chip in range(chips):
+        column = pl.multiple_of((chip * CORES + core) * columns, columns)
+        down_loads.append(
+            local(down_partial.at[:, pl.ds(column, columns)], down_own.at[chip], 1 + chips + chip)
+        )
+    base = 1 + 2 * chips
+    up_loads += [
+        local(up_master_far, up_master, base),
+        local(up_first_far, up_first, base + 1),
+        local(up_second_far, up_second, base + 2),
+    ]
+    down_loads += [
+        local(down_master_far, down_master, base + 3),
+        local(down_first_far, down_first, base + 4),
+        local(down_second_far, down_second, base + 5),
+    ]
+    base += 6
+
     partners = (
         [at_plane(1), at_plane(-1)]
         + [at_line(k) for k in range(1, lines)]
@@ -151,6 +214,7 @@
         copy.start()
         down_swap.append(copy)
 
+    tokens_load.wait()
     for s in range(group * lines):
         slabs[s] = tokens[:, s * slab : (s + 1) * slab]
     for line in range(lines):
@@ -170,25 +234,26 @@
 
     up_moves, down_moves = [], []
 
-    def pair_sum(partial, pair, chip, extent):
-        column = pl.multiple_of((chip * CORES + core) * extent, extent)
-        return partial[:, pl.ds(column, extent)].astype(jnp.float32) + pair[chip].astype(
-            jnp.float32
-        )
-
+    def pair_sum(own, pair, chip):
+        return own[chip].astype(jnp.float32) + pair[chip].astype(jnp.float32)
+
+    for copy in up_loads:
+        copy.wait()
     for copy in up_swap:
         copy.wait_recv()
     for k in range(1, chips):
         chip = (x + k) % chips
-        up_out[k] = pair_sum(up_partial, up_pair, chip, width).astype(jnp.bfloat16)
+        up_out[k] = pair_sum(up_own, up_pair, chip).astype(jnp.bfloat16)
         copy = copies.make(up_out.at[k], up_in.at[k], at_dp(chip * CORES + core))
         copy.start()
         up_moves.append(copy)
+    for copy in down_loads:
+        copy.wait()
     for copy in down_swap:
         copy.wait_recv()
     for k in range(1, chips):
         chip = (x + k) % chips
-        down_out[k] = pair_sum(down_partial, down_pair, chip, columns).astype(jnp.bfloat16)
+        down_out[k] = pair_sum(down_own, down_pair, chip).astype(jnp.bfloat16)
         copy = copies.make(down_out.at[k], down_in.at[k], at_dp(chip * CORES + core))
         copy.start()
         down_moves.append(copy)
@@ -202,7 +267,7 @@
     label = lax.broadcasted_iota(jnp.int32, totals.shape, 1)
     row_count = jnp.sum(jnp.where(label == owner, totals, 0.0))
 
-    up_total = pair_sum(up_partial, up_pair, x, width)
+    up_total = pair_sum(up_own, up_pair, x)
     for copy in up_moves:
         copy.wait_recv()
     for k in range(1, chips):
@@ -251,9 +316,10 @@
             meet((z + step) % planes)
 
     send(up_ring, 1)
+    writes = [local(up_update, up_update_far, base)]
     partial_units[...] = jnp.zeros_like(partial_units)
 
-    down_total = pair_sum(down_partial, down_pair, x, columns)
+    down_total = pair_sum(down_own, down_pair, x)
     for copy in down_moves:
         copy.wait_recv()
     for k in range(1, chips):
@@ -262,6 +328,7 @@
         down_total / row_count, down_master[...], down_first[...], down_second[...]
     )
     down_update[...] = update
+    writes.append(local(down_update, down_update_far, base + 1))
     down_all[z] = new.astype(jnp.bfloat16)
 
     for copy in token_moves:
@@ -360,9 +427,11 @@
     for k in range(1, lines):
         result = result + back_in[k].astype(jnp.float32)
     decoded[...] = result.astype(jnp.bfloat16)
-
-    for copy in copies.open:
-        copy.wait_send()
+    writes.append(local(decoded, decoded_far, base + 2))
+    for copy in writes:
+        copy.wait()
+
+    copies.drain()
 
 
 def per_device(
@@ -410,6 +479,14 @@
         + (LINES - 1)
     )
     scratch = [
+        pltpu.VMEM((rows, model), bf16),
+        pltpu.VMEM((chips, slab, width), bf16),
+        pltpu.VMEM((chips, units, columns), bf16),
+    ]
+    for _ in range(4):
+        scratch += [pltpu.VMEM((slab, width), f32), pltpu.VMEM((units, columns), f32)]
+    scratch += [
+        pltpu.VMEM((rows, columns), bf16),
         pltpu.VMEM((group * LINES, rows, slab), bf16),
         pltpu.VMEM((LINES, group, rows, slab), bf16),
         pltpu.VMEM((LINES, group, rows, slab), bf16),
@@ -435,8 +512,10 @@
         pltpu.VMEM((LINES, rows, columns), bf16),
         pltpu.SemaphoreType.DMA((copies,)),
         pltpu.SemaphoreType.DMA((copies,)),
+        pltpu.SemaphoreType.DMA((2 * chips + 10,)),
     ]
     vmem = pl.BlockSpec(memory_space=pltpu.VMEM)
+    hbm = pl.BlockSpec(memory_space=pltpu.HBM)
     sizes = (planes, LINES, chips, group, rows, slab, width, units, columns)
     up_update, down_update, decoded = pl.pallas_call(
         functools.partial(kernel, sizes),
@@ -445,11 +524,11 @@
             jax.ShapeDtypeStruct((units, columns), f32),
             jax.ShapeDtypeStruct((rows, columns), bf16),
         ),
-        in_specs=[pl.BlockSpec(memory_space=pltpu.SMEM)] + [vmem] * 11,
-        out_specs=(vmem, vmem, vmem),
+        in_specs=[pl.BlockSpec(memory_space=pltpu.SMEM), vmem, vmem] + [hbm] * 9,
+        out_specs=(hbm, hbm, hbm),
         scratch_shapes=scratch,
         compiler_params=pltpu.CompilerParams(
-            collective_id=0, has_side_effects=True, vmem_limit_bytes=48 * 1024 * 1024
+            collective_id=0, has_side_effects=True, vmem_limit_bytes=64 * 1024 * 1024
         ),
         cost_estimate=pl.CostEstimate(
             flops=2 * 2 * LINES * rows * planes * slab * width,
@@ -458,9 +537,9 @@
         ),
     )(
         owner_key,
-        tokens.reshape(rows, model),
         gates,
         counts,
+        tokens.reshape(rows, model),
         up_partial[0, 0],
         down_partial[0, 0],
         up_master[0],

time: 104 us -> 98.1 us (0.943)
  the two profiles are of different devices: /device:TPU:32 before, /device:TPU:1 now
where the time goes in v3:
time: 98.1 us; the launch traced here: 96.4 us
  Pallas kernels  89.1 us (91%)
  local copies, waits for them, and re-layouts  5.89 us (6%)
  between operations  1.35 us (1%)
    pallas_call x1, Pallas kernels, per_device(): pl.pallas_call(functools.partial(kernel, sizes), out_shape=(jax.ShapeDtyp...  89.1 us
    unnamed x13, local copies, waits for them, and re-layouts  4.57 us

profile of v3, /device:TPU:1, one launch (start us, length us, event | category | flops | bytes accessed | tf_op | source)
XLA Modules:
  0.0 96.4 jit_solution(17476785451260364862)
XLA Ops:
  1.3 0.0 copy-start.3
  1.3 0.0 copy-start.2
  1.3 0.7 copy-done.3
  2.0 0.0 copy-done.2
  2.0 0.0 copy-start.4
  2.0 0.1 select_reduce_fusion
  2.1 0.6 copy-done.4
  2.7 0.6 pad.9.counts
  3.3 0.1 copy.18
  3.4 0.6 pad.8.gates
  4.0 89.1 %shard_map.148 = (f32[448,128]{1,0:T(8,128)}, f32[64,896]{1,0:T(8,128)}, bf16[64,896]{1,0:T(8,128)(2,1)}) custom-call(s32[1]{0:T(128)} %copy.22.key_ref, f32[64,128]{1,0:T(8,128)} %pad.8.gates, s32[8,128]{1,0:T(8,128)} %pad.9.counts, bf16[64,7168]{1,0:T(8,128)(2,1)} %bitcast.18, bf16[448,1024]{1,0:T(8,128)(2,1)} %bitcast.19, bf16[64,7168]{1,0:T(8,128)(2,1)} %bitcast.20, ...), custom_call_target="tpu_custom_call" | custom-call | flops 939524096 | bytes 6291456 | tf_op jit(solution)/shard_map/pallas_call | solution.py:520
  93.1 0.0 copy-start
  93.1 1.7 %copy.23 = f32[1,448,128]{2,1,0:T(8,128)} copy(f32[1,448,128]{2,1,0:T(8,128)} %bitcast.22) | data formatting | bytes 458752
  94.8 0.0 copy-done
  94.8 0.0 copy-start.1
  94.8 0.7 copy.24
  95.5 0.3 copy-done.1
  95.8 0.6 copy.25
  (1 shorter events, 0.0 us)
Async XLA Ops:
  1.3 0.7 copy-start.3
  1.3 0.7 copy-start.2
  2.0 0.7 copy-start.4
  93.1 1.7 %copy-start = (f32[64,896]{1,0:T(8,128)S(1)}, f32[64,896]{1,0:T(8,128)}, u32[]{:S(2)}) copy-start(f32[64,896]{1,0:T(8,128)} %get-tuple-element.7) | copy-start | bytes 688132
  94.8 1.0 %copy-start.1 = (bf16[64,896]{1,0:T(8,128)(2,1)S(1)}, bf16[64,896]{1,0:T(8,128)(2,1)}, u32[]{:S(2)}) copy-start(bf16[64,896]{1,0:T(8,128)(2,1)} %get-tuple-element.8) | copy-start | bytes 344068

commit v4 on v3

--- a/solution.py
+++ b/solution.py
@@ -120,6 +120,7 @@
     units_in,
     units_all,
     units_flat,
+    back_sum,
     back_out,
     back_in,
     send_sems,
@@ -195,12 +196,18 @@
 
     copies = Copies(send_sems, recv_sems)
 
-    up_swap, down_swap = [], []
-    for chip in range(chips):
-        column = pl.multiple_of((chip * CORES + 1 - core) * width, width)
-        copy = copies.make(up_partial.at[:, pl.ds(column, width)], up_pair.at[chip], at_dp(twin))
-        copy.start()
-        up_swap.append(copy)
+    halves = [pl.ds(part * (slab // 2), slab // 2) for part in range(2)]
+    up_swap, down_swap = [[], []], []
+    for part in range(2):
+        for chip in range(chips):
+            column = pl.multiple_of((chip * CORES + 1 - core) * width, width)
+            copy = copies.make(
+                up_partial.at[halves[part], pl.ds(column, width)],
+                up_pair.at[chip, halves[part]],
+                at_dp(twin),
+            )
+            copy.start()
+            up_swap[part].append(copy)
     counts_moves = []
     for k in range(1, dp_size):
         copy = copies.make(counts, counts_in.at[k], at_dp((dp + k) % dp_size))
@@ -213,6 +220,24 @@
         )
         copy.start()
         down_swap.append(copy)
+
+    up_moves, down_moves = [[], []], []
+    for copy in up_loads[:chips]:
+        copy.wait()
+    for part in range(2):
+        for copy in up_swap[part]:
+            copy.wait_recv()
+        for k in range(1, chips):
+            chip = (x + k) % chips
+            total = up_own[chip, halves[part]].astype(jnp.float32) + up_pair[
+                chip, halves[part]
+            ].astype(jnp.float32)
+            up_out[k, halves[part]] = total.astype(jnp.bfloat16)
+            copy = copies.make(
+                up_out.at[k, halves[part]], up_in.at[k, halves[part]], at_dp(chip * CORES + core)
+            )
+            copy.start()
+            up_moves[part].append(copy)
 
     tokens_load.wait()
     for s in range(group * lines):
@@ -221,42 +246,64 @@
         for plane in range(group):
             which = jnp.bitwise_xor(plane, key_plane) * lines + jnp.bitwise_xor(line, key_line)
             tok_out[line, plane] = slabs[which]
-    token_moves = []
+    share = pl.ds(pl.multiple_of(core * (rows // 2), rows // 2), rows // 2)
+    token_moves, gate_moves = [], []
     for k in range(1, lines):
-        copy = copies.make(tok_out.at[(y + k) % lines], tok_in.at[y], at_line(k))
+        copy = copies.make(tok_out.at[(y + k) % lines, :, share], tok_in.at[y, :, share], at_line(k))
         copy.start()
         token_moves.append(copy)
         copy = copies.make(gates, gates_in.at[y], at_line(k))
         copy.start()
-        token_moves.append(copy)
+        gate_moves.append(copy)
     tok_in[y] = tok_out[y]
     gates_in[y] = gates[...]
 
-    up_moves, down_moves = [], []
-
-    def pair_sum(own, pair, chip):
-        return own[chip].astype(jnp.float32) + pair[chip].astype(jnp.float32)
-
-    for copy in up_loads:
-        copy.wait()
-    for copy in up_swap:
-        copy.wait_recv()
-    for k in range(1, chips):
-        chip = (x + k) % chips
-        up_out[k] = pair_sum(up_own, up_pair, chip).astype(jnp.bfloat16)
-        copy = copies.make(up_out.at[k], up_in.at[k], at_dp(chip * CORES + core))
-        copy.start()
-        up_moves.append(copy)
-    for copy in down_loads:
-        copy.wait()
-    for copy in down_swap:
-        copy.wait_recv()
-    for k in range(1, chips):
-        chip = (x + k) % chips
-        down_out[k] = pair_sum(down_own, down_pair, chip).astype(jnp.bfloat16)
-        copy = copies.make(down_out.at[k], down_in.at[k], at_dp(chip * CORES + core))
-        copy.start()
-        down_moves.append(copy)
+    farthest = planes // 2
+
+    def ring(blocks, parts):
+        steps = []
+        for step in range(1, farthest + 1):
+            made = {}
+            for at, (row, column, last_way) in enumerate(parts):
+                for way in (1, -1):
+                    if step == farthest and way != last_way:
+                        continue
+                    block = (z - way * (step - 1) + planes) % planes
+                    ref = blocks.at[block, row, column]
+                    made[at, way] = copies.make(ref, ref, at_plane(way))
+            steps.append(made)
+        return steps
+
+    def send(steps, parts):
+        for (at, _), copy in steps[0].items():
+            if at in parts:
+                copy.start()
+
+    def pass_on(steps, step):
+        onward = steps[step] if step < farthest else {}
+        for place_of, copy in steps[step - 1].items():
+            copy.wait_recv()
+            if place_of in onward:
+                onward[place_of].start()
+
+    quarter = slab // 4
+    whole = pl.ds(0, width)
+    up_ring = ring(
+        up_all,
+        [(pl.ds(at * quarter, quarter), whole, 1 if at % 2 == 0 else -1) for at in range(4)],
+    )
+    left = columns - columns // 256 * 128
+    sides = [(0, left), (left, columns - left)]
+    down_rings = [
+        ring(
+            down_all,
+            [
+                (pl.ds(at * (units // 2), units // 2), pl.ds(low_column, extent), 1 - 2 * at)
+                for at in range(2)
+            ],
+        )
+        for low_column, extent in sides
+    ]
 
     for copy in counts_moves:
         copy.wait_recv()
@@ -266,44 +313,53 @@
     owner = jnp.bitwise_xor(z // group, key_group)
     label = lax.broadcasted_iota(jnp.int32, totals.shape, 1)
     row_count = jnp.sum(jnp.where(label == owner, totals, 0.0))
-
-    up_total = pair_sum(up_own, up_pair, x)
-    for copy in up_moves:
+    for copy in up_loads[chips:]:
+        copy.wait()
+    for part in range(2):
+        half = halves[part]
+        total = up_own[x, half].astype(jnp.float32) + up_pair[x, half].astype(jnp.float32)
+        for copy in up_moves[part]:
+            copy.wait_recv()
+        for k in range(1, chips):
+            total = total + up_in[k, half].astype(jnp.float32)
+        update, new = adamw_step(total / row_count, up_master[half], up_first[half], up_second[half])
+        up_update[half] = update
+        up_all[z, half] = new.astype(jnp.bfloat16)
+        send(up_ring, (2 * part, 2 * part + 1))
+        if part == 0:
+            for copy in down_loads:
+                copy.wait()
+            for copy in down_swap:
+                copy.wait_recv()
+            for k in range(1, chips):
+                chip = (x + k) % chips
+                total = down_own[chip].astype(jnp.float32) + down_pair[chip].astype(jnp.float32)
+                down_out[k] = total.astype(jnp.bfloat16)
+                copy = copies.make(down_out.at[k], down_in.at[k], at_dp(chip * CORES + core))
+                copy.start()
+                down_moves.append(copy)
+    writes = [local(up_update, up_update_far, base)]
+
+    pass_on(up_ring, 1)
+    total = down_own[x].astype(jnp.float32) + down_pair[x].astype(jnp.float32)
+    for copy in down_moves:
         copy.wait_recv()
     for k in range(1, chips):
-        up_total = up_total + up_in[k].astype(jnp.float32)
-    update, new = adamw_step(up_total / row_count, up_master[...], up_first[...], up_second[...])
-    up_update[...] = update
-    up_all[z] = new.astype(jnp.bfloat16)
-
-    farthest = planes // 2
-
-    def ring(blocks, extent):
-        half = extent // 2
-        steps = {}
-        for step in range(1, farthest + 1):
-            steps[step] = []
-            for way, part in ((1, 0), (-1, 1), (1, 1), (-1, 0)):
-                if step == farthest and (way == 1) != (part == 0):
-                    continue
-                block = (z - way * (step - 1) + planes) % planes
-                ref = blocks.at[block, pl.ds(part * half, half)]
-                steps[step].append(copies.make(ref, ref, at_plane(way)))
-        return steps
-
-    def send(steps, step):
-        for copy in steps[step]:
-            copy.start()
-
-    def pass_on(steps, step):
-        onward = steps.get(step + 1, [])
-        for at, copy in enumerate(steps[step]):
-            copy.wait_recv()
-            if at < len(onward):
-                onward[at].start()
-
-    up_ring = ring(up_all, slab)
-    down_ring = ring(down_all, units)
+        total = total + down_in[k].astype(jnp.float32)
+    update, new = adamw_step(total / row_count, down_master[...], down_first[...], down_second[...])
+    down_update[...] = update
+    down_all[z] = new.astype(jnp.bfloat16)
+    writes.append(local(down_update, down_update_far, base + 1))
+    partial_units[...] = jnp.zeros_like(partial_units)
+    pass_on(up_ring, 2)
+    twin_moves = []
+    for k in range(1, lines):
+        token_moves[k - 1].wait_recv()
+        gate_moves[k - 1].wait_recv()
+        held = tok_in.at[(y - k + lines) % lines, :, share]
+        copy = copies.make(held, held, at_dp(twin))
+        copy.start()
+        twin_moves.append(copy)
 
     def meet(block):
         held = tok_in[:, block % group].reshape(lines * rows, slab)
@@ -315,33 +371,28 @@
         if step < farthest:
             meet((z + step) % planes)
 
-    send(up_ring, 1)
-    writes = [local(up_update, up_update_far, base)]
-    partial_units[...] = jnp.zeros_like(partial_units)
-
-    down_total = pair_sum(down_own, down_pair, x)
-    for copy in down_moves:
+    def down_pass(first, second):
+        if first:
+            pass_on(down_rings[0], first)
+        if second:
+            pass_on(down_rings[1], second)
+
+    pass_on(up_ring, 3)
+    send(down_rings[0], (0, 1))
+    for copy in twin_moves:
         copy.wait_recv()
-    for k in range(1, chips):
-        down_total = down_total + down_in[k].astype(jnp.float32)
-    update, new = adamw_step(
-        down_total / row_count, down_master[...], down_first[...], down_second[...]
-    )
-    down_update[...] = update
-    writes.append(local(down_update, down_update_far, base + 1))
-    down_all[z] = new.astype(jnp.bfloat16)
-
-    for copy in token_moves:
-        copy.wait_recv()
-    pass_on(up_ring, 1)
     meet(z)
     meet_step(1)
-    for step in range(2, farthest - 1):
+    pass_on(up_ring, 4)
+    send(down_rings[1], (0, 1))
+    meet_step(2)
+    meet_step(3)
+    for step in range(5, farthest):
+        down_pass(step - 4, step - 5)
         pass_on(up_ring, step)
-        meet_step(step)
-    send(down_ring, 1)
-    pass_on(up_ring, farthest - 1)
+        meet_step(step - 1)
     meet_step(farthest - 1)
+    down_pass(farthest - 4, farthest - 5)
     pass_on(up_ring, farthest)
     meet_step(farthest)
 
@@ -351,8 +402,6 @@
     )
     swap = copies.make(swap_out, swap_in, at_dp(twin))
     swap.start()
-    pass_on(down_ring, 1)
-    swap.wait_recv()
 
     def blocks_of(value, first):
         upper, lower = value[:, :rows], value[:, rows:]
@@ -360,6 +409,7 @@
         unit_blocks[first + 1] = jnp.where(low, turn(upper), lower)
 
     blocks_of(partial_units[:, pl.ds(pl.multiple_of(core * half, half), half)], 2 * core)
+    swap.wait_recv()
     blocks_of(swap_in[...].astype(jnp.float32), 2 * (1 - core))
     unit_moves = []
     for k in range(1, lines):
@@ -368,7 +418,7 @@
         copy = copies.make(units_out.at[k], units_in.at[k], at_line(k))
         copy.start()
         unit_moves.append(copy)
-    pass_on(down_ring, 2)
+    down_pass(farthest - 3, farthest - 4)
     summed = unit_blocks[jnp.bitwise_xor(y, key_line)]
     for copy in unit_moves:
         copy.wait_recv()
@@ -380,13 +430,24 @@
         gate = jnp.where(low, upper, lower)
         units_all[dp, g] = (jax.nn.silu(summed[g]) * gate).astype(jnp.bfloat16)
     spread = []
-    for k in range(1, dp_size):
-        copy = copies.make(units_all.at[dp], units_all.at[dp], at_dp((dp + k) % dp_size))
+    for k in range(1, chips):
+        copy = copies.make(
+            units_all.at[dp], units_all.at[dp], at_dp((x + k) % chips * CORES + core)
+        )
         copy.start()
         spread.append(copy)
-    for step in range(3, farthest - 1):
-        pass_on(down_ring, step)
-    for copy in spread:
+    copy = copies.make(units_all.at[dp], units_all.at[dp], at_dp(twin))
+    copy.start()
+    twin_moves = [copy]
+    down_pass(farthest - 2, farthest - 3)
+    for k in range(1, chips):
+        spread[k - 1].wait_recv()
+        held = units_all.at[(x - k + chips) % chips * CORES + core]
+        copy = copies.make(held, held, at_dp(twin))
+        copy.start()
+        twin_moves.append(copy)
+    down_pass(farthest - 1, farthest - 2)
+    for copy in twin_moves:
         copy.wait_recv()
 
     for g in range(EXPERTS):
@@ -406,22 +467,30 @@
                 units_flat[row + rows : row + half, column : column + 2 * units] = jnp.where(
                     low, turn(even), odd
                 ).astype(jnp.bfloat16)
-    for step in range(farthest - 1, farthest + 1):
-        pass_on(down_ring, step)
-
-    flat_down = down_all[...].reshape(planes * units, columns)
-
-    def produce(line):
-        held = units_flat[pl.ds(pl.multiple_of(line * rows, rows), rows)]
-        return jnp.dot(held, flat_down, preferred_element_type=jnp.float32)
 
     back_moves = []
-    for k in range(1, lines):
-        back_out[k] = produce((y + k) % lines).astype(jnp.bfloat16)
-        copy = copies.make(back_out.at[k], back_in.at[k], at_line(k))
-        copy.start()
-        back_moves.append(copy)
-    result = produce(y)
+    for side, (low_column, extent) in enumerate(sides):
+        if side == 0:
+            down_pass(farthest, farthest - 1)
+        else:
+            down_pass(0, farthest)
+        side_columns = pl.ds(low_column, extent)
+        product = jnp.dot(
+            units_flat[...],
+            down_all[:, :, side_columns].reshape(planes * units, extent),
+            preferred_element_type=jnp.float32,
+        ).reshape(lines, rows, extent)
+        back_sum[:, :, side_columns] = product
+        back_out[:, :, side_columns] = product.astype(jnp.bfloat16)
+        for k in range(1, lines):
+            copy = copies.make(
+                back_out.at[(y + k) % lines, :, side_columns],
+                back_in.at[k, :, side_columns],
+                at_line(k),
+            )
+            copy.start()
+            back_moves.append(copy)
+    result = back_sum[y]
     for copy in back_moves:
         copy.wait_recv()
     for k in range(1, lines):
@@ -468,15 +537,15 @@
     counts = jnp.pad(counts, ((0, 7), (0, 128 - EXPERTS)))
 
     copies = (
-        2 * chips
+        3 * chips
         + (dp_size - 1)
-        + 2 * (LINES - 1)
-        + 2 * (chips - 1)
-        + 2 * 2 * (planes - 1)
+        + 3 * (LINES - 1)
+        + 3 * (chips - 1)
+        + (4 + 2 + 2) * (planes - 1)
         + 1
         + (LINES - 1)
-        + (dp_size - 1)
-        + (LINES - 1)
+        + 2 * chips - 1
+        + 2 * (LINES - 1)
     )
     scratch = [
         pltpu.VMEM((rows, model), bf16),
@@ -508,6 +577,7 @@
         pltpu.VMEM((LINES, EXPERTS, rows, 2 * units), bf16),
         pltpu.VMEM((dp_size, EXPERTS, rows, 2 * units), bf16),
         pltpu.VMEM((LINES * rows, planes * units), bf16),
+        pltpu.VMEM((LINES, rows, columns), f32),
         pltpu.VMEM((LINES, rows, columns), bf16),
         pltpu.VMEM((LINES, rows, columns), bf16),
         pltpu.SemaphoreType.DMA((copies,)),

time: 98.1 us -> 89.2 us (0.909); the launches traced: 96.4 us -> 88.8 us
  Pallas kernels: 89.1 us -> 81.5 us
    pallas_call x1, Pallas kernels: 89.1 us -> 81.5 us  [per_device(): pl.pallas_call(functools.partial(kernel, sizes), out_shape=(jax.ShapeDtyp...]
where the time goes in v4:
time: 89.2 us; the launch traced here: 88.8 us
  Pallas kernels  81.5 us (91%)
  local copies, waits for them, and re-layouts  5.89 us (7%)
  between operations  1.35 us (2%)
    pallas_call x1, Pallas kernels, per_device(): pl.pallas_call(functools.partial(kernel, sizes), out_shape=(jax.ShapeDtyp...  81.5 us
    unnamed x13, local copies, waits for them, and re-layouts  4.57 us

profile of v4, /device:TPU:1, one launch (start us, length us, event | category | flops | bytes accessed | tf_op | source)
XLA Modules:
  0.0 88.8 jit_solution(13436438890114752673)
XLA Ops:
  1.3 0.0 copy-start.3
  1.3 0.0 copy-start.2
  1.3 0.7 copy-done.3
  2.0 0.0 copy-done.2
  2.0 0.0 copy-start.4
  2.0 0.1 select_reduce_fusion
  2.1 0.6 copy-done.4
  2.7 0.6 pad.9.counts
  3.3 0.1 copy.18
  3.4 0.6 pad.8.gates
  4.0 81.5 %shard_map.148 = (f32[448,128]{1,0:T(8,128)}, f32[64,896]{1,0:T(8,128)}, bf16[64,896]{1,0:T(8,128)(2,1)}) custom-call(s32[1]{0:T(128)} %copy.22.key_ref, f32[64,128]{1,0:T(8,128)} %pad.8.gates, s32[8,128]{1,0:T(8,128)} %pad.9.counts, bf16[64,7168]{1,0:T(8,128)(2,1)} %bitcast.18, bf16[448,1024]{1,0:T(8,128)(2,1)} %bitcast.19, bf16[64,7168]{1,0:T(8,128)(2,1)} %bitcast.20, ...), custom_call_target="tpu_custom_call" | custom-call | flops 939524096 | bytes 6291456 | tf_op jit(solution)/shard_map/pallas_call | solution.py:590
  85.5 0.0 copy-start
  85.5 1.7 %copy.23 = f32[1,448,128]{2,1,0:T(8,128)} copy(f32[1,448,128]{2,1,0:T(8,128)} %bitcast.22) | data formatting | bytes 458752
  87.2 0.0 copy-done
  87.2 0.0 copy-start.1
  87.2 0.7 copy.24
  87.8 0.3 copy-done.1
  88.1 0.6 copy.25
  (1 shorter events, 0.0 us)
Async XLA Ops:
  1.3 0.7 copy-start.3
  1.3 0.7 copy-start.2
  2.0 0.7 copy-start.4
  85.5 1.7 %copy-start = (f32[64,896]{1,0:T(8,128)S(1)}, f32[64,896]{1,0:T(8,128)}, u32[]{:S(2)}) copy-start(f32[64,896]{1,0:T(8,128)} %get-tuple-element.7) | copy-start | bytes 688132
  87.2 1.0 %copy-start.1 = (bf16[64,896]{1,0:T(8,128)(2,1)S(1)}, bf16[64,896]{1,0:T(8,128)(2,1)}, u32[]{:S(2)}) copy-start(bf16[64,896]{1,0:T(8,128)(2,1)} %get-tuple-element.8) | copy-start | bytes 344068

commit v5 on v4

--- a/solution.py
+++ b/solution.py
@@ -73,8 +73,9 @@
 def kernel(
     sizes,
     key_ref,
-    gates,
-    counts,
+    routes,
+    mix_weights,
+    own_counts,
     tokens_far,
     up_partial,
     down_partial,
@@ -102,7 +103,9 @@
     slabs,
     tok_out,
     tok_in,
+    gates,
     gates_in,
+    counts,
     counts_in,
     up_pair,
     down_pair,
@@ -154,34 +157,6 @@
     def turn(value):
         return pltpu.roll(value, units, value.ndim - 1)
 
-    def local(src, dst, at):
-        copy = pltpu.make_async_copy(src, dst, local_sems.at[at])
-        copy.start()
-        return copy
-
-    tokens_load = local(tokens_far, tokens, 0)
-    up_loads, down_loads = [], []
-    for chip in range(chips):
-        column = pl.multiple_of((chip * CORES + core) * width, width)
-        up_loads.append(local(up_partial.at[:, pl.ds(column, width)], up_own.at[chip], 1 + chip))
-    for chip in range(chips):
-        column = pl.multiple_of((chip * CORES + core) * columns, columns)
-        down_loads.append(
-            local(down_partial.at[:, pl.ds(column, columns)], down_own.at[chip], 1 + chips + chip)
-        )
-    base = 1 + 2 * chips
-    up_loads += [
-        local(up_master_far, up_master, base),
-        local(up_first_far, up_first, base + 1),
-        local(up_second_far, up_second, base + 2),
-    ]
-    down_loads += [
-        local(down_master_far, down_master, base + 3),
-        local(down_first_far, down_first, base + 4),
-        local(down_second_far, down_second, base + 5),
-    ]
-    base += 6
-
     partners = (
         [at_plane(1), at_plane(-1)]
         + [at_line(k) for k in range(1, lines)]
@@ -192,6 +167,13 @@
         pl.semaphore_signal(
             barrier, inc=1, device_id=partner, device_id_type=pl.DeviceIdType.MESH
         )
+
+    def local(src, dst, at):
+        copy = pltpu.make_async_copy(src, dst, local_sems.at[at])
+        copy.start()
+        return copy
+
+    up_load = local(up_partial, up_own, 0)
     pl.semaphore_wait(barrier, len(partners))
 
     copies = Copies(send_sems, recv_sems)
@@ -208,6 +190,42 @@
             )
             copy.start()
             up_swap[part].append(copy)
+
+    up_moves, down_moves = [[], []], []
+
+    def up_sum(chip, part):
+        column = pl.multiple_of((chip * CORES + core) * width, width)
+        return up_own[halves[part], pl.ds(column, width)].astype(jnp.float32) + up_pair[
+            chip, halves[part]
+        ].astype(jnp.float32)
+
+    def down_sum(chip):
+        column = pl.multiple_of((chip * CORES + core) * columns, columns)
+        return down_own[:, pl.ds(column, columns)].astype(jnp.float32) + down_pair[chip].astype(
+            jnp.float32
+        )
+
+    up_load.wait()
+    for part in range(2):
+        for copy in up_swap[part]:
+            copy.wait_recv()
+        for k in range(1, chips):
+            chip = (x + k) % chips
+            up_out[k, halves[part]] = up_sum(chip, part).astype(jnp.bfloat16)
+            copy = copies.make(
+                up_out.at[k, halves[part]], up_in.at[k, halves[part]], at_dp(chip * CORES + core)
+            )
+            copy.start()
+            up_moves[part].append(copy)
+
+    tokens_load = local(tokens_far, tokens, 1)
+    up_loads = [
+        local(up_master_far, up_master, 2),
+        local(up_first_far, up_first, 3),
+        local(up_second_far, up_second, 4),
+    ]
+    counts[...] = jnp.zeros_like(counts)
+    counts[0:1, 0:EXPERTS] = own_counts[...]
     counts_moves = []
     for k in range(1, dp_size):
         copy = copies.make(counts, counts_in.at[k], at_dp((dp + k) % dp_size))
@@ -220,24 +238,21 @@
         )
         copy.start()
         down_swap.append(copy)
-
-    up_moves, down_moves = [[], []], []
-    for copy in up_loads[:chips]:
-        copy.wait()
-    for part in range(2):
-        for copy in up_swap[part]:
-            copy.wait_recv()
-        for k in range(1, chips):
-            chip = (x + k) % chips
-            total = up_own[chip, halves[part]].astype(jnp.float32) + up_pair[
-                chip, halves[part]
-            ].astype(jnp.float32)
-            up_out[k, halves[part]] = total.astype(jnp.bfloat16)
-            copy = copies.make(
-                up_out.at[k, halves[part]], up_in.at[k, halves[part]], at_dp(chip * CORES + core)
-            )
-            copy.start()
-            up_moves[part].append(copy)
+    down_loads = [
+        local(down_partial, down_own, 5),
+        local(down_master_far, down_master, 6),
+        local(down_first_far, down_first, 7),
+        local(down_second_far, down_second, 8),
+    ]
+    base = 9
+
+    gates[...] = jnp.zeros_like(gates)
+    for g in range(EXPERTS):
+        chosen = routes[...] == jnp.bitwise_xor(g, key_group)
+        gate = jnp.sum(jnp.where(chosen, mix_weights[...], 0.0), axis=1)
+        for step in range(gate.shape[0]):
+            extent = gate.shape[1]
+            gates[g : g + 1, step * extent : (step + 1) * extent] = gate[step : step + 1]
 
     tokens_load.wait()
     for s in range(group * lines):
@@ -313,11 +328,11 @@
     owner = jnp.bitwise_xor(z // group, key_group)
     label = lax.broadcasted_iota(jnp.int32, totals.shape, 1)
     row_count = jnp.sum(jnp.where(label == owner, totals, 0.0))
-    for copy in up_loads[chips:]:
+    for copy in up_loads:
         copy.wait()
     for part in range(2):
         half = halves[part]
-        total = up_own[x, half].astype(jnp.float32) + up_pair[x, half].astype(jnp.float32)
+        total = up_sum(x, part)
         for copy in up_moves[part]:
             copy.wait_recv()
         for k in range(1, chips):
@@ -333,15 +348,14 @@
                 copy.wait_recv()
             for k in range(1, chips):
                 chip = (x + k) % chips
-                total = down_own[chip].astype(jnp.float32) + down_pair[chip].astype(jnp.float32)
-                down_out[k] = total.astype(jnp.bfloat16)
+                down_out[k] = down_sum(chip).astype(jnp.bfloat16)
                 copy = copies.make(down_out.at[k], down_in.at[k], at_dp(chip * CORES + core))
                 copy.start()
                 down_moves.append(copy)
     writes = [local(up_update, up_update_far, base)]
 
     pass_on(up_ring, 1)
-    total = down_own[x].astype(jnp.float32) + down_pair[x].astype(jnp.float32)
+    total = down_sum(x)
     for copy in down_moves:
         copy.wait_recv()
     for k in range(1, chips):
@@ -424,10 +438,9 @@
         copy.wait_recv()
     for k in range(1, lines):
         summed = summed + units_in[k].astype(jnp.float32)
+    upper, lower = gates_in[2 * core].T, gates_in[2 * core + 1].T
     for g in range(EXPERTS):
-        upper = gates_in[2 * core][:, g : g + 1]
-        lower = gates_in[2 * core + 1][:, g : g + 1]
-        gate = jnp.where(low, upper, lower)
+        gate = jnp.where(low, upper[:rows, g : g + 1], lower[:rows, g : g + 1])
         units_all[dp, g] = (jax.nn.silu(summed[g]) * gate).astype(jnp.bfloat16)
     spread = []
     for k in range(1, chips):
@@ -503,6 +516,25 @@
     copies.drain()
 
 
+def hand_out(a, b, c, a_out, b_out, c_out, a_held, b_held, c_held, sems):
+    held = (a_held, b_held, c_held)
+    reads = [
+        pltpu.make_async_copy(src, dst, sems.at[at])
+        for at, (src, dst) in enumerate(zip((a, b, c), held))
+    ]
+    writes = [
+        pltpu.make_async_copy(src, dst, sems.at[3 + at])
+        for at, (src, dst) in enumerate(zip(held, (a_out, b_out, c_out)))
+    ]
+    for copy in reads:
+        copy.start()
+    for read, write in zip(reads, writes):
+        read.wait()
+        write.start()
+    for copy in writes:
+        copy.wait()
+
+
 def per_device(
     tokens,
     routes,
@@ -528,14 +560,6 @@
     units, columns = down_master.shape[1:]
     bf16, f32 = jnp.bfloat16, jnp.float32
 
-    holder = jnp.bitwise_xor(
-        jnp.arange(EXPERTS, dtype=jnp.int32), owner_key[0] // (LINES * group)
-    )
-    matches = routes[..., None] == holder
-    gates = jnp.sum(jnp.where(matches, mix_weights[..., None], 0.0), axis=2)
-    gates = jnp.pad(gates.reshape(rows, EXPERTS), ((0, 0), (0, 128 - EXPERTS)))
-    counts = jnp.pad(counts, ((0, 7), (0, 128 - EXPERTS)))
-
     copies = (
         3 * chips
         + (dp_size - 1)
@@ -549,8 +573,8 @@
     )
     scratch = [
         pltpu.VMEM((rows, model), bf16),
-        pltpu.VMEM((chips, slab, width), bf16),
-        pltpu.VMEM((chips, units, columns), bf16),
+        pltpu.VMEM(up_partial.shape[2:], bf16),
+        pltpu.VMEM(down_partial.shape[2:], bf16),
     ]
     for _ in range(4):
         scratch += [pltpu.VMEM((slab, width), f32), pltpu.VMEM((units, columns), f32)]
@@ -559,7 +583,9 @@
         pltpu.VMEM((group * LINES, rows, slab), bf16),
         pltpu.VMEM((LINES, group, rows, slab), bf16),
         pltpu.VMEM((LINES, group, rows, slab), bf16),
-        pltpu.VMEM((LINES, rows, 128), f32),
+        pltpu.VMEM((8, 128), f32),
+        pltpu.VMEM((LINES, 8, 128), f32),
+        pltpu.VMEM((8, 128), jnp.int32),
         pltpu.VMEM((dp_size, 8, 128), jnp.int32),
         pltpu.VMEM((chips, slab, width), bf16),
         pltpu.VMEM((chips, units, columns), bf16),
@@ -582,7 +608,7 @@
         pltpu.VMEM((LINES, rows, columns), bf16),
         pltpu.SemaphoreType.DMA((copies,)),
         pltpu.SemaphoreType.DMA((copies,)),
-        pltpu.SemaphoreType.DMA((2 * chips + 10,)),
+        pltpu.SemaphoreType.DMA((12,)),
     ]
     vmem = pl.BlockSpec(memory_space=pltpu.VMEM)
     hbm = pl.BlockSpec(memory_space=pltpu.HBM)
@@ -594,7 +620,7 @@
             jax.ShapeDtypeStruct((units, columns), f32),
             jax.ShapeDtypeStruct((rows, columns), bf16),
         ),
-        in_specs=[pl.BlockSpec(memory_space=pltpu.SMEM), vmem, vmem] + [hbm] * 9,
+        in_specs=[pl.BlockSpec(memory_space=pltpu.SMEM), vmem, vmem, vmem] + [hbm] * 9,
         out_specs=(hbm, hbm, hbm),
         scratch_shapes=scratch,
         compiler_params=pltpu.CompilerParams(
@@ -607,7 +633,8 @@
         ),
     )(
         owner_key,
-        gates,
+        routes.transpose(0, 2, 1),
+        mix_weights.transpose(0, 2, 1),
         counts,
         tokens.reshape(rows, model),
         up_partial[0, 0],
@@ -619,6 +646,16 @@
         up_second[0],
         down_second[0],
     )
+    results = (up_update, down_update, decoded)
+    up_update, down_update, decoded = pl.pallas_call(
+        hand_out,
+        out_shape=tuple(jax.ShapeDtypeStruct(r.shape, r.dtype) for r in results),
+        in_specs=[hbm] * 3,
+        out_specs=(hbm,) * 3,
+        scratch_shapes=[pltpu.VMEM(r.shape, r.dtype) for r in results]
+        + [pltpu.SemaphoreType.DMA((6,))],
+        compiler_params=pltpu.CompilerParams(vmem_limit_bytes=64 * 1024 * 1024),
+    )(*results)
     return (up_update[None], down_update[None], decoded.reshape(steps, rows_dev, columns))
 
 

time: 89.2 us -> 87.8 us (0.984)
  local copies, waits for them, and re-layouts: 5.89 us -> 0 us
  Pallas kernels: 81.5 us -> 86 us
    unnamed x13 -> x0, local copies, waits for them, and re-layouts: 4.57 us -> none
    pallas_call x1, Pallas kernels: 81.5 us -> 84.2 us  [per_device(): pl.pallas_call(functools.partial(kernel, sizes), out_shape=(jax.ShapeDtyp...]
    pallas_call x0 -> x1, Pallas kernels: none -> 1.82 us  [per_device(): pl.pallas_call(hand_out, out_shape=tuple((jax.ShapeDtypeStruct(r.shape, r...]
    pad x2 -> x0, local copies, waits for them, and re-layouts: 1.22 us -> none  [the longest x1 0.62 us: per_device(): gates = jnp.pad(gates.reshape(rows, EXPERTS), ((0, 0), (0, 128 - EXPERTS)))]
where the time goes in v5:
time: 87.8 us; the launch traced here: 87.3 us
  Pallas kernels  86 us (98%)
  between operations  1.29 us (1%)
    pallas_call x1, Pallas kernels, per_device(): pl.pallas_call(functools.partial(kernel, sizes), out_shape=(jax.ShapeDtyp...  84.2 us
    pallas_call x1, Pallas kernels, per_device(): pl.pallas_call(hand_out, out_shape=tuple((jax.ShapeDtypeStruct(r.shape, r...  1.82 us

profile of v5, /device:TPU:1, one launch (start us, length us, event | category | flops | bytes accessed | tf_op | source)
XLA Modules:
  0.0 87.3 jit_solution(17770457525677768083)
XLA Ops:
  1.3 84.2 %shard_map.148 = (f32[448,128]{1,0:T(8,128)}, f32[64,896]{1,0:T(8,128)}, bf16[64,896]{1,0:T(8,128)(2,1)}) custom-call(s32[1]{0:T(128)S(6)} %copy.16.key_ref, s32[2,2,32]{2,1,0:T(2,128)} %bitcast.23, f32[2,2,32]{2,1,0:T(2,128)} %bitcast.24, s32[1,4]{1,0:T(1,128)} %own_counts.1, bf16[64,7168]{1,0:T(8,128)(2,1)} %bitcast.14, bf16[448,1024]{1,0:T(8,128)(2,1)} %bitcast.15, ...), custom_call_target="tpu_custom_call" | custom-call | flops 939524096 | bytes 6291456 | tf_op jit(solution)/shard_map/pallas_call | solution.py:616
  85.5 1.8 %shard_map.149 = (f32[448,128]{1,0:T(8,128)}, f32[64,896]{1,0:T(8,128)}, bf16[64,896]{1,0:T(8,128)(2,1)}) custom-call(f32[448,128]{1,0:T(8,128)} %get-tuple-element.9.a, f32[64,896]{1,0:T(8,128)} %get-tuple-element.10.b, bf16[64,896]{1,0:T(8,128)(2,1)} %get-tuple-element.11.c), custom_call_target="tpu_custom_call" | custom-call | tf_op jit(solution)/shard_map/pallas_call | solution.py:650

commit v6 on v5

--- a/solution.py
+++ b/solution.py
@@ -87,7 +87,8 @@
     down_second_far,
     up_update_far,
     down_update_far,
-    decoded_far,
+    own_far,
+    back_far,
     tokens,
     up_own,
     down_own,
@@ -99,7 +100,6 @@
     down_second,
     up_update,
     down_update,
-    decoded,
     slabs,
     tok_out,
     tok_in,
@@ -125,7 +125,6 @@
     units_flat,
     back_sum,
     back_out,
-    back_in,
     send_sems,
     recv_sems,
     local_sems,
@@ -178,25 +177,27 @@
 
     copies = Copies(send_sems, recv_sems)
 
-    halves = [pl.ds(part * (slab // 2), slab // 2) for part in range(2)]
-    up_swap, down_swap = [[], []], []
-    for part in range(2):
+    parts = 4
+    quarter = slab // parts
+    bands = [pl.ds(part * quarter, quarter) for part in range(parts)]
+    up_swap, down_swap = [[] for _ in bands], []
+    for part in range(parts):
         for chip in range(chips):
             column = pl.multiple_of((chip * CORES + 1 - core) * width, width)
             copy = copies.make(
-                up_partial.at[halves[part], pl.ds(column, width)],
-                up_pair.at[chip, halves[part]],
+                up_partial.at[bands[part], pl.ds(column, width)],
+                up_pair.at[chip, bands[part]],
                 at_dp(twin),
             )
             copy.start()
             up_swap[part].append(copy)
 
-    up_moves, down_moves = [[], []], []
+    up_moves, down_moves = [[] for _ in bands], []
 
     def up_sum(chip, part):
         column = pl.multiple_of((chip * CORES + core) * width, width)
-        return up_own[halves[part], pl.ds(column, width)].astype(jnp.float32) + up_pair[
-            chip, halves[part]
+        return up_own[bands[part], pl.ds(column, width)].astype(jnp.float32) + up_pair[
+            chip, bands[part]
         ].astype(jnp.float32)
 
     def down_sum(chip):
@@ -205,18 +206,22 @@
             jnp.float32
         )
 
-    up_load.wait()
-    for part in range(2):
+    def up_send(part):
         for copy in up_swap[part]:
             copy.wait_recv()
         for k in range(1, chips):
-            chip = (x + k) % chips
-            up_out[k, halves[part]] = up_sum(chip, part).astype(jnp.bfloat16)
+            up_out[k, bands[part]] = up_sum((x + k) % chips, part).astype(jnp.bfloat16)
+        for k in range(1, chips):
             copy = copies.make(
-                up_out.at[k, halves[part]], up_in.at[k, halves[part]], at_dp(chip * CORES + core)
+                up_out.at[k, bands[part]],
+                up_in.at[k, bands[part]],
+                at_dp((x + k) % chips * CORES + core),
             )
             copy.start()
             up_moves[part].append(copy)
+
+    up_load.wait()
+    up_send(0)
 
     tokens_load = local(tokens_far, tokens, 1)
     up_loads = [
@@ -224,6 +229,7 @@
         local(up_first_far, up_first, 3),
         local(up_second_far, up_second, 4),
     ]
+    up_send(1)
     counts[...] = jnp.zeros_like(counts)
     counts[0:1, 0:EXPERTS] = own_counts[...]
     counts_moves = []
@@ -231,6 +237,7 @@
         copy = copies.make(counts, counts_in.at[k], at_dp((dp + k) % dp_size))
         copy.start()
         counts_moves.append(copy)
+    up_send(2)
     for chip in range(chips):
         column = pl.multiple_of((chip * CORES + 1 - core) * columns, columns)
         copy = copies.make(
@@ -245,6 +252,7 @@
         local(down_second_far, down_second, 8),
     ]
     base = 9
+    up_send(3)
 
     gates[...] = jnp.zeros_like(gates)
     for g in range(EXPERTS):
@@ -301,12 +309,8 @@
             if place_of in onward:
                 onward[place_of].start()
 
-    quarter = slab // 4
     whole = pl.ds(0, width)
-    up_ring = ring(
-        up_all,
-        [(pl.ds(at * quarter, quarter), whole, 1 if at % 2 == 0 else -1) for at in range(4)],
-    )
+    up_ring = ring(up_all, [(band, whole, 1 - 2 * (at % 2)) for at, band in enumerate(bands)])
     left = columns - columns // 256 * 128
     sides = [(0, left), (left, columns - left)]
     down_rings = [
@@ -330,18 +334,17 @@
     row_count = jnp.sum(jnp.where(label == owner, totals, 0.0))
     for copy in up_loads:
         copy.wait()
-    for part in range(2):
-        half = halves[part]
+    for part, band in enumerate(bands):
         total = up_sum(x, part)
         for copy in up_moves[part]:
             copy.wait_recv()
         for k in range(1, chips):
-            total = total + up_in[k, half].astype(jnp.float32)
-        update, new = adamw_step(total / row_count, up_master[half], up_first[half], up_second[half])
-        up_update[half] = update
-        up_all[z, half] = new.astype(jnp.bfloat16)
-        send(up_ring, (2 * part, 2 * part + 1))
-        if part == 0:
+            total = total + up_in[k, band].astype(jnp.float32)
+        update, new = adamw_step(total / row_count, up_master[band], up_first[band], up_second[band])
+        up_update[band] = update
+        up_all[z, band] = new.astype(jnp.bfloat16)
+        send(up_ring, (part,))
+        if part == 1:
             for copy in down_loads:
                 copy.wait()
             for copy in down_swap:
@@ -391,146 +394,206 @@
         if second:
             pass_on(down_rings[1], second)
 
+    half = lines * rows // 2
+    mine = pl.ds(pl.multiple_of(core * half, half), half)
+    other = pl.ds(pl.multiple_of((1 - core) * half, half), half)
+    order = (0, 1, 3, 2)
+
+    def holder(at):
+        return (z // group + order[at]) % EXPERTS
+
+    class Units:
+        def __init__(self, first, count):
+            self.ats, self.span = range(first, first + count), pl.ds(first, count)
+
+        def swap(self):
+            for at in self.ats:
+                swap_out[at] = partial_units[holder(at), other].astype(jnp.bfloat16)
+            self.swapped = copies.make(
+                swap_out.at[self.span], swap_in.at[self.span], at_dp(twin)
+            )
+            self.swapped.start()
+
+        def along_lines(self):
+            def blocks_of(value, at, first):
+                upper, lower = value[:rows], value[rows:]
+                unit_blocks[first, at] = jnp.where(low, upper, turn(lower))
+                unit_blocks[first + 1, at] = jnp.where(low, turn(upper), lower)
+
+            for at in self.ats:
+                blocks_of(partial_units[holder(at), mine], at, 2 * core)
+            self.swapped.wait_recv()
+            for at in self.ats:
+                blocks_of(swap_in[at].astype(jnp.float32), at, 2 * (1 - core))
+            self.moves = []
+            for k in range(1, lines):
+                block = jnp.bitwise_xor((y + k) % lines, key_line)
+                for at in self.ats:
+                    units_out[k, at] = unit_blocks[block, at].astype(jnp.bfloat16)
+                copy = copies.make(
+                    units_out.at[k, self.span], units_in.at[k, self.span], at_line(k)
+                )
+                copy.start()
+                self.moves.append(copy)
+
+        def over_dp(self):
+            for copy in self.moves:
+                copy.wait_recv()
+            upper, lower = gates_in[2 * core].T[:rows], gates_in[2 * core + 1].T[:rows]
+            label = lax.broadcasted_iota(jnp.int32, upper.shape, 1)
+            for at in self.ats:
+                summed = unit_blocks[jnp.bitwise_xor(y, key_line), at]
+                for k in range(1, lines):
+                    summed = summed + units_in[k, at].astype(jnp.float32)
+                gate = [
+                    jnp.sum(jnp.where(label == holder(at), value, 0.0), axis=1, keepdims=True)
+                    for value in (upper, lower)
+                ]
+                gated = jax.nn.silu(summed) * jnp.where(low, gate[0], gate[1])
+                units_all[dp, at] = gated.astype(jnp.bfloat16)
+            self.moves = []
+            held = units_all.at[dp, self.span]
+            for k in range(1, chips):
+                copy = copies.make(held, held, at_dp((x + k) % chips * CORES + core))
+                copy.start()
+                self.moves.append(copy)
+            self.twin_moves = [copies.make(held, held, at_dp(twin))]
+            self.twin_moves[0].start()
+
+        def to_twin(self):
+            for k in range(1, chips):
+                self.moves[k - 1].wait_recv()
+                held = units_all.at[(x - k + chips) % chips * CORES + core, self.span]
+                copy = copies.make(held, held, at_dp(twin))
+                copy.start()
+                self.twin_moves.append(copy)
+
+        def landed(self):
+            for copy in self.twin_moves:
+                copy.wait_recv()
+
+        def flat(self):
+            for at in self.ats:
+                for pair in range(group // 2):
+                    column = (at * group + 2 * pair) * units
+                    for owner_core in range(CORES):
+                        even, odd = (
+                            units_all[
+                                jnp.bitwise_xor(2 * pair + n, key_plane) * CORES + owner_core, at
+                            ].astype(jnp.float32)
+                            for n in range(2)
+                        )
+                        row = owner_core * half
+                        units_flat[row : row + rows, column : column + 2 * units] = jnp.where(
+                            low, even, turn(odd)
+                        ).astype(jnp.bfloat16)
+                        units_flat[row + rows : row + half, column : column + 2 * units] = (
+                            jnp.where(low, turn(even), odd).astype(jnp.bfloat16)
+                        )
+
+    near, far = Units(0, EXPERTS - 1), Units(EXPERTS - 1, 1)
+    lag_left, lag_right = 2, 3
+
+    def down_pass(step):
+        for blocks, lag in ((down_rings[0], lag_left), (down_rings[1], lag_right)):
+            if 1 <= step - lag <= farthest:
+                pass_on(blocks, step - lag)
+            if step == lag:
+                send(blocks, (0, 1))
+
+    down_pass(2)
     pass_on(up_ring, 3)
-    send(down_rings[0], (0, 1))
+    down_pass(3)
     for copy in twin_moves:
         copy.wait_recv()
     meet(z)
     meet_step(1)
     pass_on(up_ring, 4)
-    send(down_rings[1], (0, 1))
+    down_pass(4)
     meet_step(2)
     meet_step(3)
     for step in range(5, farthest):
-        down_pass(step - 4, step - 5)
         pass_on(up_ring, step)
+        down_pass(step)
         meet_step(step - 1)
     meet_step(farthest - 1)
-    down_pass(farthest - 4, farthest - 5)
+    near.swap()
+    near.along_lines()
     pass_on(up_ring, farthest)
     meet_step(farthest)
-
-    half = lines * rows // 2
-    swap_out[...] = partial_units[:, pl.ds(pl.multiple_of((1 - core) * half, half), half)].astype(
-        jnp.bfloat16
-    )
-    swap = copies.make(swap_out, swap_in, at_dp(twin))
-    swap.start()
-
-    def blocks_of(value, first):
-        upper, lower = value[:, :rows], value[:, rows:]
-        unit_blocks[first] = jnp.where(low, upper, turn(lower))
-        unit_blocks[first + 1] = jnp.where(low, turn(upper), lower)
-
-    blocks_of(partial_units[:, pl.ds(pl.multiple_of(core * half, half), half)], 2 * core)
-    swap.wait_recv()
-    blocks_of(swap_in[...].astype(jnp.float32), 2 * (1 - core))
-    unit_moves = []
-    for k in range(1, lines):
-        line = (y + k) % lines
-        units_out[k] = unit_blocks[jnp.bitwise_xor(line, key_line)].astype(jnp.bfloat16)
-        copy = copies.make(units_out.at[k], units_in.at[k], at_line(k))
-        copy.start()
-        unit_moves.append(copy)
-    down_pass(farthest - 3, farthest - 4)
-    summed = unit_blocks[jnp.bitwise_xor(y, key_line)]
-    for copy in unit_moves:
-        copy.wait_recv()
-    for k in range(1, lines):
-        summed = summed + units_in[k].astype(jnp.float32)
-    upper, lower = gates_in[2 * core].T, gates_in[2 * core + 1].T
-    for g in range(EXPERTS):
-        gate = jnp.where(low, upper[:rows, g : g + 1], lower[:rows, g : g + 1])
-        units_all[dp, g] = (jax.nn.silu(summed[g]) * gate).astype(jnp.bfloat16)
-    spread = []
-    for k in range(1, chips):
-        copy = copies.make(
-            units_all.at[dp], units_all.at[dp], at_dp((x + k) % chips * CORES + core)
-        )
-        copy.start()
-        spread.append(copy)
-    copy = copies.make(units_all.at[dp], units_all.at[dp], at_dp(twin))
-    copy.start()
-    twin_moves = [copy]
-    down_pass(farthest - 2, farthest - 3)
-    for k in range(1, chips):
-        spread[k - 1].wait_recv()
-        held = units_all.at[(x - k + chips) % chips * CORES + core]
-        copy = copies.make(held, held, at_dp(twin))
-        copy.start()
-        twin_moves.append(copy)
-    down_pass(farthest - 1, farthest - 2)
-    for copy in twin_moves:
-        copy.wait_recv()
-
-    for g in range(EXPERTS):
-        for pair in range(group // 2):
-            column = (g * group + 2 * pair) * units
-            for owner_core in range(CORES):
-                even = units_all[
-                    jnp.bitwise_xor(2 * pair, key_plane) * CORES + owner_core, g
-                ].astype(jnp.float32)
-                odd = units_all[
-                    jnp.bitwise_xor(2 * pair + 1, key_plane) * CORES + owner_core, g
-                ].astype(jnp.float32)
-                row = owner_core * half
-                units_flat[row : row + rows, column : column + 2 * units] = jnp.where(
-                    low, even, turn(odd)
-                ).astype(jnp.bfloat16)
-                units_flat[row + rows : row + half, column : column + 2 * units] = jnp.where(
-                    low, turn(even), odd
-                ).astype(jnp.bfloat16)
+    far.swap()
+    far.along_lines()
+    near.over_dp()
+    down_pass(farthest)
+    far.over_dp()
+    down_pass(farthest + 1)
+    near.to_twin()
+    far.to_twin()
+    for step in range(farthest + 2, farthest + lag_left + 1):
+        down_pass(step)
+    near.landed()
+    far.landed()
+    near.flat()
+    far.flat()
 
     back_moves = []
     for side, (low_column, extent) in enumerate(sides):
-        if side == 0:
-            down_pass(farthest, farthest - 1)
-        else:
-            down_pass(0, farthest)
+        if side == 1:
+            for step in range(farthest + lag_left + 1, farthest + lag_right + 1):
+                down_pass(step)
         side_columns = pl.ds(low_column, extent)
-        product = jnp.dot(
-            units_flat[...],
-            down_all[:, :, side_columns].reshape(planes * units, extent),
-            preferred_element_type=jnp.float32,
-        ).reshape(lines, rows, extent)
+        product = jnp.zeros((lines * rows, extent), jnp.float32)
+        for at in range(EXPERTS):
+            held = down_all[pl.ds(holder(at) * group, group), :, side_columns]
+            product = product + jnp.dot(
+                units_flat[:, at * group * units : (at + 1) * group * units],
+                held.reshape(group * units, extent),
+                preferred_element_type=jnp.float32,
+            )
+        product = product.reshape(lines, rows, extent)
         back_sum[:, :, side_columns] = product
         back_out[:, :, side_columns] = product.astype(jnp.bfloat16)
         for k in range(1, lines):
             copy = copies.make(
                 back_out.at[(y + k) % lines, :, side_columns],
-                back_in.at[k, :, side_columns],
+                back_far.at[k - 1, :, side_columns],
                 at_line(k),
             )
             copy.start()
             back_moves.append(copy)
-    result = back_sum[y]
+    writes.append(local(back_sum.at[y], own_far, base + 2))
     for copy in back_moves:
         copy.wait_recv()
-    for k in range(1, lines):
-        result = result + back_in[k].astype(jnp.float32)
-    decoded[...] = result.astype(jnp.bfloat16)
-    writes.append(local(decoded, decoded_far, base + 2))
     for copy in writes:
         copy.wait()
 
     copies.drain()
 
 
-def hand_out(a, b, c, a_out, b_out, c_out, a_held, b_held, c_held, sems):
-    held = (a_held, b_held, c_held)
+def hand_out(a, b, own, back, a_out, b_out, out, a_held, b_held, own_held, back_held, held, sems):
     reads = [
         pltpu.make_async_copy(src, dst, sems.at[at])
-        for at, (src, dst) in enumerate(zip((a, b, c), held))
+        for at, (src, dst) in enumerate(
+            ((own, own_held), (back, back_held), (a, a_held), (b, b_held))
+        )
     ]
     writes = [
-        pltpu.make_async_copy(src, dst, sems.at[3 + at])
-        for at, (src, dst) in enumerate(zip(held, (a_out, b_out, c_out)))
+        pltpu.make_async_copy(src, dst, sems.at[4 + at])
+        for at, (src, dst) in enumerate(((held, out), (a_held, a_out), (b_held, b_out)))
     ]
     for copy in reads:
         copy.start()
-    for read, write in zip(reads, writes):
-        read.wait()
-        write.start()
+    reads[0].wait()
+    reads[1].wait()
+    result = own_held[...]
+    for k in range(back_held.shape[0]):
+        result = result + back_held[k].astype(jnp.float32)
+    held[...] = result.astype(held.dtype)
+    writes[0].start()
+    reads[2].wait()
+    writes[1].start()
+    reads[3].wait()
+    writes[2].start()
     for copy in writes:
         copy.wait()
 
@@ -561,14 +624,14 @@
     bf16, f32 = jnp.bfloat16, jnp.float32
 
     copies = (
-        3 * chips
+        (4 + 1) * chips
         + (dp_size - 1)
         + 3 * (LINES - 1)
-        + 3 * (chips - 1)
+        + (4 + 1) * (chips - 1)
         + (4 + 2 + 2) * (planes - 1)
-        + 1
-        + (LINES - 1)
-        + 2 * chips - 1
+        + 2 * 1
+        + 2 * (LINES - 1)
+        + 2 * (2 * chips - 1)
         + 2 * (LINES - 1)
     )
     scratch = [
@@ -579,7 +642,6 @@
     for _ in range(4):
         scratch += [pltpu.VMEM((slab, width), f32), pltpu.VMEM((units, columns), f32)]
     scratch += [
-        pltpu.VMEM((rows, columns), bf16),
         pltpu.VMEM((group * LINES, rows, slab), bf16),
         pltpu.VMEM((LINES, group, rows, slab), bf16),
         pltpu.VMEM((LINES, group, rows, slab), bf16),
@@ -605,7 +667,6 @@
         pltpu.VMEM((LINES * rows, planes * units), bf16),
         pltpu.VMEM((LINES, rows, columns), f32),
         pltpu.VMEM((LINES, rows, columns), bf16),
-        pltpu.VMEM((LINES, rows, columns), bf16),
         pltpu.SemaphoreType.DMA((copies,)),
         pltpu.SemaphoreType.DMA((copies,)),
         pltpu.SemaphoreType.DMA((12,)),
@@ -613,15 +674,16 @@
     vmem = pl.BlockSpec(memory_space=pltpu.VMEM)
     hbm = pl.BlockSpec(memory_space=pltpu.HBM)
     sizes = (planes, LINES, chips, group, rows, slab, width, units, columns)
-    up_update, down_update, decoded = pl.pallas_call(
+    results = pl.pallas_call(
         functools.partial(kernel, sizes),
         out_shape=(
             jax.ShapeDtypeStruct((slab, width), f32),
             jax.ShapeDtypeStruct((units, columns), f32),
-            jax.ShapeDtypeStruct((rows, columns), bf16),
+            jax.ShapeDtypeStruct((rows, columns), f32),
+            jax.ShapeDtypeStruct((LINES - 1, rows, columns), bf16),
         ),
         in_specs=[pl.BlockSpec(memory_space=pltpu.SMEM), vmem, vmem, vmem] + [hbm] * 9,
-        out_specs=(hbm, hbm, hbm),
+        out_specs=(hbm,) * 4,
         scratch_shapes=scratch,
         compiler_params=pltpu.CompilerParams(
             collective_id=0, has_side_effects=True, vmem_limit_bytes=64 * 1024 * 1024
@@ -646,14 +708,14 @@
         up_second[0],
         down_second[0],
     )
-    results = (up_update, down_update, decoded)
+    out_shapes = [((slab, width), f32), ((units, columns), f32), ((rows, columns), bf16)]
     up_update, down_update, decoded = pl.pallas_call(
         hand_out,
-        out_shape=tuple(jax.ShapeDtypeStruct(r.shape, r.dtype) for r in results),
-        in_specs=[hbm] * 3,
+        out_shape=tuple(jax.ShapeDtypeStruct(*shape) for shape in out_shapes),
+        in_specs=[hbm] * 4,
         out_specs=(hbm,) * 3,
         scratch_shapes=[pltpu.VMEM(r.shape, r.dtype) for r in results]
-        + [pltpu.SemaphoreType.DMA((6,))],
+        + [pltpu.VMEM((rows, columns), bf16), pltpu.SemaphoreType.DMA((7,))],
         compiler_params=pltpu.CompilerParams(vmem_limit_bytes=64 * 1024 * 1024),
     )(*results)
     return (up_update[None], down_update[None], decoded.reshape(steps, rows_dev, columns))

time: 87.8 us -> 84.4 us (0.961)
  Pallas kernels: 86 us -> 82.9 us
    pallas_call x1, Pallas kernels: 84.2 us -> 80.9 us  [per_device(): pl.pallas_call(functools.partial(kernel, sizes), out_shape=(jax.ShapeDtyp...]
where the time goes in v6:
time: 84.4 us; the launch traced here: 84.2 us
  Pallas kernels  82.9 us (98%)
  between operations  1.29 us (2%)
    pallas_call x1, Pallas kernels, per_device(): pl.pallas_call(functools.partial(kernel, sizes), out_shape=(jax.ShapeDtyp...  80.9 us
    pallas_call x1, Pallas kernels, per_device(): pl.pallas_call(hand_out, out_shape=tuple((jax.ShapeDtypeStruct(*shape) fo...  2.02 us

profile of v6, /device:TPU:1, one launch (start us, length us, event | category | flops | bytes accessed | tf_op | source)
XLA Modules:
  0.0 84.2 jit_solution(5311163800494873366)
XLA Ops:
  1.3 80.9 %shard_map.148 = (f32[448,128]{1,0:T(8,128)}, f32[64,896]{1,0:T(8,128)}, f32[64,896]{1,0:T(8,128)}, bf16[3,64,896]{2,1,0:T(8,128)(2,1)}) custom-call(s32[1]{0:T(128)S(6)} %copy.16.key_ref, s32[2,2,32]{2,1,0:T(2,128)} %bitcast.23, f32[2,2,32]{2,1,0:T(2,128)} %bitcast.24, s32[1,4]{1,0:T(1,128)} %own_counts.1, bf16[64,7168]{1,0:T(8,128)(2,1)} %bitcast.14, ...), custom_call_target="tpu_custom_call" | custom-call | flops 939524096 | bytes 6291456 | tf_op jit(solution)/shard_map/pallas_call | solution.py:677
  82.2 2.0 %shard_map.149 = (f32[448,128]{1,0:T(8,128)}, f32[64,896]{1,0:T(8,128)}, bf16[64,896]{1,0:T(8,128)(2,1)}) custom-call(f32[448,128]{1,0:T(8,128)} %get-tuple-element.10.a, f32[64,896]{1,0:T(8,128)} %get-tuple-element.11.b, f32[64,896]{1,0:T(8,128)} %get-tuple-element.12.own, bf16[3,64,896]{2,1,0:T(8,128)(2,1)} %get-tuple-element.13.back), custom_call_target="tpu_custom_call" | custom-call | tf_op jit(solution)/shard_map/pallas_call | solution.py:712

commit v7 on v6

--- a/solution.py
+++ b/solution.py
@@ -451,16 +451,19 @@
                 ]
                 gated = jax.nn.silu(summed) * jnp.where(low, gate[0], gate[1])
                 units_all[dp, at] = gated.astype(jnp.bfloat16)
+            held = units_all.at[dp, self.span]
+            if len(self.ats) == 1:
+                targets = [(dp + k) % dp_size for k in range(1, dp_size)]
+            else:
+                targets = [(x + k) % chips * CORES + core for k in range(1, chips)] + [twin]
             self.moves = []
-            held = units_all.at[dp, self.span]
-            for k in range(1, chips):
-                copy = copies.make(held, held, at_dp((x + k) % chips * CORES + core))
+            for target in targets:
+                copy = copies.make(held, held, at_dp(target))
                 copy.start()
                 self.moves.append(copy)
-            self.twin_moves = [copies.make(held, held, at_dp(twin))]
-            self.twin_moves[0].start()
 
         def to_twin(self):
+            self.twin_moves = self.moves[chips - 1 :]
             for k in range(1, chips):
                 self.moves[k - 1].wait_recv()
                 held = units_all.at[(x - k + chips) % chips * CORES + core, self.span]
@@ -469,7 +472,7 @@
                 self.twin_moves.append(copy)
 
         def landed(self):
-            for copy in self.twin_moves:
+            for copy in self.moves if len(self.ats) == 1 else self.twin_moves:
                 copy.wait_recv()
 
         def flat(self):
@@ -492,7 +495,7 @@
                         )
 
     near, far = Units(0, EXPERTS - 1), Units(EXPERTS - 1, 1)
-    lag_left, lag_right = 2, 3
+    lag_left, lag_right = 3, 3
 
     def down_pass(step):
         for blocks, lag in ((down_rings[0], lag_left), (down_rings[1], lag_right)):
@@ -522,13 +525,12 @@
     pass_on(up_ring, farthest)
     meet_step(farthest)
     far.swap()
+    down_pass(farthest)
     far.along_lines()
     near.over_dp()
-    down_pass(farthest)
     far.over_dp()
     down_pass(farthest + 1)
     near.to_twin()
-    far.to_twin()
     for step in range(farthest + 2, farthest + lag_left + 1):
         down_pass(step)
     near.landed()
@@ -631,7 +633,7 @@
         + (4 + 2 + 2) * (planes - 1)
         + 2 * 1
         + 2 * (LINES - 1)
-        + 2 * (2 * chips - 1)
+        + (2 * chips - 1) + (dp_size - 1)
         + 2 * (LINES - 1)
     )
     scratch = [

time: 84.4 us -> 83.9 us (level)
  no operation moved by 1% of the time
where the time goes in v7:
time: 83.9 us; the launch traced here: 83.7 us
  Pallas kernels  82.4 us (98%)
  between operations  1.29 us (2%)
    pallas_call x1, Pallas kernels, per_device(): pl.pallas_call(functools.partial(kernel, sizes), out_shape=(jax.ShapeDtyp...  80.4 us
    pallas_call x1, Pallas kernels, per_device(): pl.pallas_call(hand_out, out_shape=tuple((jax.ShapeDtypeStruct(*shape) fo...  2.02 us

profile of v7, /device:TPU:1, one launch (start us, length us, event | category | flops | bytes accessed | tf_op | source)
XLA Modules:
  0.0 83.7 jit_solution(13917986983536766486)
XLA Ops:
  1.3 80.4 %shard_map.148 = (f32[448,128]{1,0:T(8,128)}, f32[64,896]{1,0:T(8,128)}, f32[64,896]{1,0:T(8,128)}, bf16[3,64,896]{2,1,0:T(8,128)(2,1)}) custom-call(s32[1]{0:T(128)S(6)} %copy.16.key_ref, s32[2,2,32]{2,1,0:T(2,128)} %bitcast.23, f32[2,2,32]{2,1,0:T(2,128)} %bitcast.24, s32[1,4]{1,0:T(1,128)} %own_counts.1, bf16[64,7168]{1,0:T(8,128)(2,1)} %bitcast.14, ...), custom_call_target="tpu_custom_call" | custom-call | flops 939524096 | bytes 6291456 | tf_op jit(solution)/shard_map/pallas_call | solution.py:679
  81.7 2.0 %shard_map.149 = (f32[448,128]{1,0:T(8,128)}, f32[64,896]{1,0:T(8,128)}, bf16[64,896]{1,0:T(8,128)(2,1)}) custom-call(f32[448,128]{1,0:T(8,128)} %get-tuple-element.10.a, f32[64,896]{1,0:T(8,128)} %get-tuple-element.11.b, f32[64,896]{1,0:T(8,128)} %get-tuple-element.12.own, bf16[3,64,896]{2,1,0:T(8,128)(2,1)} %get-tuple-element.13.back), custom_call_target="tpu_custom_call" | custom-call | tf_op jit(solution)/shard_map/pallas_call | solution.py:714
